TPU v7x, 512 devices: a whole 4x8x8 slice. The times are simulated.
512 devices in a mesh: seq: 64 (over y, x, core), tok: 8 (over z).
Axes of the slice: x: 4, y: 8, z: 8, core: 2. Of those that a mesh axis runs over, the one named last changes fastest.
Arguments:
- queries: bfloat16 [65536, 2048], P(('seq', 'tok')), may hold values from -6 to 6
- key_vectors: bfloat16 [65536, 2048], P(('seq', 'tok')), may hold values from -6 to 6
- value_vectors: bfloat16 [65536, 2048], P(('seq', 'tok')), may hold values from -6 to 6
- grad_output: bfloat16 [65536, 2048], P(('seq', 'tok')), may hold values from -8192 to 8192
- memory: float32 [64, 16, 128, 128], P('seq', 'tok'), may hold values from -7596.0074 to 7596.0074
- normalizer: float32 [64, 16, 128], P('seq', 'tok'), may hold values from 256 to 411648
- gate_logit: float32 [16], replicated, may hold values from 4 to 7
Outputs:
- grad_queries: bfloat16 [65536, 2048], P(('seq', 'tok'))
- grad_keys: bfloat16 [65536, 2048], P(('seq', 'tok'))
- grad_values: bfloat16 [65536, 2048], P(('seq', 'tok'))
All inputs are finite; a program needn't handle non-finite values.
Results may differ from a plain program's by a relative error of at most 0.0022.
Values may be sent and summed in bfloat16 or wider, within the bound.
No kernel may reach another device: no remote copies, remote signals or barrier semaphores. Data moves between devices by JAX's collectives and lax.ppermute only.
A program may use at most 64 MiB of HBM per device.

v0:
```python
import jax
import jax.numpy as jnp
from jax import lax
from jax.sharding import PartitionSpec as P

HIGHEST = lax.Precision.HIGHEST
NEG_LARGE = -1e30


def feature_map(inputs):
    lower = jnp.exp(jnp.minimum(inputs, 0.0))
    positive = inputs > 0
    return (jnp.where(positive, inputs + 1.0, lower), jnp.where(positive, 1.0, lower))


def memory_read(query_rows, grad_rows, memory_slab, normal_vector, gate_value):
    features, slopes = feature_map(query_rows.astype(jnp.float32))
    numerator = jnp.dot(features, memory_slab, precision=HIGHEST)
    denominator = jnp.dot(features, normal_vector, precision=HIGHEST)
    scaled_grad = gate_value * grad_rows.astype(jnp.float32)
    grad_numerator = scaled_grad / denominator[:, None]
    grad_denominator = -jnp.sum(scaled_grad * numerator, axis=1) / (denominator * denominator)
    memory_grad = jnp.dot(features.T, grad_numerator, precision=HIGHEST)
    normal_grad = jnp.dot(grad_denominator, features, precision=HIGHEST)
    grad_features = (
        jnp.dot(grad_numerator, memory_slab.T, precision=HIGHEST)
        + grad_denominator[:, None] * normal_vector[None, :]
    )
    return (memory_grad, normal_grad, grad_features * slopes)


def memory_write(key_rows, value_rows, later_memory, later_normal):
    features, slopes = feature_map(key_rows.astype(jnp.float32))
    value_grad = jnp.dot(features, later_memory, precision=HIGHEST)
    feature_grad = (
        jnp.dot(value_rows.astype(jnp.float32), later_memory.T, precision=HIGHEST)
        + later_normal[None, :]
    )
    return (feature_grad * slopes, value_grad)


def attend_rows(query_rows, row_start, key_rows, value_rows, grad_rows, local_share, score_scale):
    scores = (
        jnp.einsum("qd,kd->qk", query_rows, key_rows, preferred_element_type=jnp.float32)
        * score_scale
    )
    positions = row_start + lax.broadcasted_iota(jnp.int32, scores.shape, 0)
    columns = lax.broadcasted_iota(jnp.int32, scores.shape, 1)
    scores = jnp.where(columns <= positions, scores, NEG_LARGE)
    highest = jnp.max(scores, axis=1, keepdims=True)
    exponent = jnp.exp(scores - highest)
    attention = exponent / jnp.sum(exponent, axis=1, keepdims=True)
    grad_attention = local_share * jnp.einsum(
        "qd,kd->qk", grad_rows, value_rows, preferred_element_type=jnp.float32
    )
    centre = jnp.sum(attention * grad_attention, axis=1, keepdims=True)
    grad_scores = (attention * (grad_attention - centre)).astype(jnp.bfloat16)
    grad_query = score_scale * jnp.dot(grad_scores, key_rows, preferred_element_type=jnp.float32)
    grad_key = score_scale * jnp.einsum(
        "qk,qd->kd", grad_scores, query_rows, preferred_element_type=jnp.float32
    )
    grad_value = local_share * jnp.einsum(
        "qk,qd->kd", attention.astype(jnp.bfloat16), grad_rows, preferred_element_type=jnp.float32
    )
    return (grad_query, grad_key, grad_value)


def body(queries, key_vectors, value_vectors, grad_output, memory, normalizer, gate_logit):
    groups = lax.axis_size("tok")
    head_total = gate_logit.shape[0]
    local_heads = head_total // groups
    head_size = memory.shape[-1]
    score_scale = head_size ** (-0.5)
    query_heads, key_heads, value_heads, grad_heads = (
        lax.all_to_all(queries, "tok", split_axis=1, concat_axis=0, tiled=True),
        lax.all_to_all(key_vectors, "tok", split_axis=1, concat_axis=0, tiled=True),
        lax.all_to_all(value_vectors, "tok", split_axis=1, concat_axis=0, tiled=True),
        lax.all_to_all(grad_output, "tok", split_axis=1, concat_axis=0, tiled=True),
    )
    seg_rows = query_heads.shape[0]
    gate_values = jax.nn.sigmoid(
        lax.dynamic_slice_in_dim(gate_logit, lax.axis_index("tok") * local_heads, local_heads)
    )

    def columns_of(array, head_index):
        return array[:, head_index * head_size : (head_index + 1) * head_size]

    memory_list = []
    normal_list = []
    query_memory = []
    for head_index in range(local_heads):
        memory_grad, normal_grad, query_part = memory_read(
            columns_of(query_heads, head_index),
            columns_of(grad_heads, head_index),
            memory[0, head_index],
            normalizer[0, head_index],
            gate_values[head_index],
        )
        memory_list.append(memory_grad)
        normal_list.append(normal_grad)
        query_memory.append(query_part)
    memory_grads = jnp.stack(memory_list)[None]
    normal_grads = jnp.stack(normal_list)[None]
    own_segment = lax.axis_index("seq")
    pieces = (
        lax.all_gather(memory_grads, "seq", axis=0, tiled=True),
        lax.all_gather(normal_grads, "seq", axis=0, tiled=True),
    )
    selected = (jnp.arange(pieces[0].shape[0]) > own_segment).astype(jnp.float32)
    later_memory = jnp.sum(pieces[0] * selected[:, None, None, None], axis=0, keepdims=True)
    later_normal = jnp.sum(pieces[1] * selected[:, None, None], axis=0, keepdims=True)
    block_rows = min(512, seg_rows)
    block_count = seg_rows // block_rows
    query_out = []
    key_out = []
    value_out = []
    for head_index in range(local_heads):
        query_head = columns_of(query_heads, head_index)
        key_head = columns_of(key_heads, head_index)
        value_head = columns_of(value_heads, head_index)
        grad_head = columns_of(grad_heads, head_index)
        local_share = 1.0 - gate_values[head_index]

        def block_step(carry, block_index):
            row_start = block_index * block_rows
            query_block = lax.dynamic_slice_in_dim(query_head, row_start, block_rows, 0)
            grad_block = lax.dynamic_slice_in_dim(grad_head, row_start, block_rows, 0)
            grad_query, grad_key, grad_value = attend_rows(
                query_block, row_start, key_head, value_head, grad_block, local_share, score_scale
            )
            return ((carry[0] + grad_key, carry[1] + grad_value), grad_query)

        empty = jnp.zeros((seg_rows, head_size), jnp.float32)
        (key_local, value_local), query_blocks = lax.scan(
            block_step, (empty, empty), jnp.arange(block_count)
        )
        query_local = query_blocks.reshape(seg_rows, head_size)
        key_write, value_write = memory_write(
            key_head, value_head, later_memory[0, head_index], later_normal[0, head_index]
        )
        query_out.append((query_local + query_memory[head_index]).astype(jnp.bfloat16))
        key_out.append((key_local + key_write).astype(jnp.bfloat16))
        value_out.append((value_local + value_write).astype(jnp.bfloat16))
    query_grads = jnp.concatenate(query_out, axis=1)
    key_grads = jnp.concatenate(key_out, axis=1)
    value_grads = jnp.concatenate(value_out, axis=1)
    result_q, result_k, result_v = (
        lax.all_to_all(query_grads, "tok", split_axis=0, concat_axis=1, tiled=True),
        lax.all_to_all(key_grads, "tok", split_axis=0, concat_axis=1, tiled=True),
        lax.all_to_all(value_grads, "tok", split_axis=0, concat_axis=1, tiled=True),
    )
    return (result_q, result_k, result_v)


def solution(mesh):
    in_specs = (
        P(("seq", "tok"), None),
        P(("seq", "tok"), None),
        P(("seq", "tok"), None),
        P(("seq", "tok"), None),
        P("seq", "tok", None, None),
        P("seq", "tok", None),
        P(),
    )
    out_specs = (P(("seq", "tok"), None), P(("seq", "tok"), None), P(("seq", "tok"), None))
    return jax.shard_map(body, mesh=mesh, in_specs=in_specs, out_specs=out_specs, check_vma=False)
```

profile of v0, /device:TPU:1, one launch (start us, length us, event | category | flops | bytes accessed | tf_op | source)
XLA Modules:
  0.0 267.8 jit_solution(14200388796689921154)
XLA Ops:
  7.2 2.1 copy.29
  9.3 11.0 %all-to-all-start = ((bf16[128,8,256]{0,2,1:T(8,128)(2,1)}), bf16[128,8,256]{0,2,1:T(8,128)(2,1)S(1)}, u32[]{:S(2)}, u32[]{:S(2)}) async-start(bf16[128,8,256]{0,2,1:T(8,128)(2,1)} %bitcast), calls=%async_computation | async-start | bytes 1048576 | tf_op jit(solution)/shard_map/all_to_all | solution.py:75
  20.3 1.0 copy.33
  21.3 17.0 %all-to-all-done = bf16[128,8,256]{0,2,1:T(8,128)(2,1)S(1)} async-done(((bf16[128,8,256]{0,2,1:T(8,128)(2,1)}), bf16[128,8,256]{0,2,1:T(8,128)(2,1)S(1)}, u32[]{:S(2)}, u32[]{:S(2)}) %all-to-all-start) | async-done | bytes 524320 | tf_op jit(solution)/shard_map/all_to_all | solution.py:75
  38.2 3.5 %all-to-all-start.2 = ((bf16[128,8,256]{0,2,1:T(8,128)(2,1)}), bf16[128,8,256]{0,2,1:T(8,128)(2,1)S(1)}, u32[]{:S(2)}, u32[]{:S(2)}) async-start(bf16[128,8,256]{0,2,1:T(8,128)(2,1)} %bitcast.5), calls=%async_computation.2 | async-start | bytes 1048576 | tf_op jit(solution)/shard_map/all_to_all | solution.py:78
  43.6 16.0 %all-to-all-done.2 = bf16[128,8,256]{0,2,1:T(8,128)(2,1)S(1)} async-done(((bf16[128,8,256]{0,2,1:T(8,128)(2,1)}), bf16[128,8,256]{0,2,1:T(8,128)(2,1)S(1)}, u32[]{:S(2)}, u32[]{:S(2)}) %all-to-all-start.2) | async-done | bytes 524320 | tf_op jit(solution)/shard_map/all_to_all | solution.py:78
  59.7 1.3 convolution_bitcast_fusion
  61.1 1.4 convolution_bitcast_fusion.1
  63.2 1.0 copy.31
  64.2 3.5 %all-to-all-start.1 = ((bf16[128,8,256]{0,2,1:T(8,128)(2,1)}), bf16[128,8,256]{0,2,1:T(8,128)(2,1)S(1)}, u32[]{:S(2)}, u32[]{:S(2)}) async-start(bf16[128,8,256]{0,2,1:T(8,128)(2,1)} %bitcast.2), calls=%async_computation.1 | async-start | bytes 1048576 | tf_op jit(solution)/shard_map/all_to_all | solution.py:76
  69.8 15.7 %all-to-all-done.1 = bf16[128,8,256]{0,2,1:T(8,128)(2,1)S(1)} async-done(((bf16[128,8,256]{0,2,1:T(8,128)(2,1)}), bf16[128,8,256]{0,2,1:T(8,128)(2,1)S(1)}, u32[]{:S(2)}, u32[]{:S(2)}) %all-to-all-start.1) | async-done | bytes 524320 | tf_op jit(solution)/shard_map/all_to_all | solution.py:76
  85.6 3.7 %all-to-all-start.3 = ((bf16[128,8,256]{2,0,1:T(8,128)(2,1)}), bf16[128,8,256]{2,0,1:T(8,128)(2,1)S(1)}, u32[]{:S(2)}, u32[]{:S(2)}) async-start(bf16[128,8,256]{2,0,1:T(8,128)(2,1)} %bitcast.177), calls=%async_computation.3 | async-start | bytes 1048576 | tf_op jit(solution)/shard_map/all_to_all | solution.py:77
  92.1 13.6 %all-to-all-done.3 = bf16[128,8,256]{2,0,1:T(8,128)(2,1)S(1)} async-done(((bf16[128,8,256]{2,0,1:T(8,128)(2,1)}), bf16[128,8,256]{2,0,1:T(8,128)(2,1)S(1)}, u32[]{:S(2)}, u32[]{:S(2)}) %all-to-all-start.3) | async-done | bytes 524320 | tf_op jit(solution)/shard_map/all_to_all | solution.py:77
  107.4 19.8 %while.30 = (s32[]{:T(128)}, f32[1024,128]{1,0:T(8,128)S(1)}, f32[1024,128]{1,0:T(8,128)}, f32[2,512,128]{2,1,0:T(8,128)}, s32[2]{0:T(128)S(1)}, /*index=5*/bf16...) while((s32[]{:T(128)}, f32[1024,128]{1,0:T(8,128)S(1)}, ...), condition=%wide.region_4.5_spmd.clone, body=%wide.region_0.4_spmd.clone.sunk | while | flops 682425344 | bytes 28863348 | solution.py:134
  108.6 1.6 fusion.216
  110.7 2.5 fusion.219
  113.2 1.1 multiply_reduce_fusion.6
  118.4 1.6 fusion.216
  120.5 2.7 fusion.219
  123.2 1.1 multiply_reduce_fusion.6
  127.2 2.1 copy.48
  129.3 1.2 copy.41
  131.3 19.9 %while.31 = (s32[]{:T(128)}, f32[1024,128]{1,0:T(8,128)S(1)}, f32[1024,128]{1,0:T(8,128)}, f32[2,512,128]{2,1,0:T(8,128)}, s32[2]{0:T(128)S(1)}, /*index=5*/bf16...) while((s32[]{:T(128)}, f32[1024,128]{1,0:T(8,128)S(1)}, ...), condition=%wide.region_10.11_spmd.clone, body=%wide.region_6.0_spmd.clone.sunk | while | flops 682425344 | bytes 28863348 | solution.py:134
  132.6 1.6 fusion.229
  134.7 2.5 fusion.232
  137.1 1.1 multiply_reduce_fusion.7
  142.4 1.6 fusion.229
  144.5 2.7 fusion.232
  147.2 1.1 multiply_reduce_fusion.7
  151.2 1.4 copy.49
  152.6 2.0 copy.54
  154.7 1.0 copy.55
  155.7 1.4 fusion.51
  157.1 1.4 fusion.50
  158.5 1.5 fusion.46
  160.0 1.4 fusion.47
  162.3 3.5 %all-to-all-start.4 = ((bf16[8,128,256]{1,2,0:T(8,128)(2,1)}), bf16[8,128,256]{1,2,0:T(8,128)(2,1)S(1)}, u32[]{:S(2)}, u32[]{:S(2)}) async-start(bf16[8,128,256]{1,2,0:T(8,128)(2,1)} %copy_bitcast_fusion.5), calls=%async_computation.4 | async-start | bytes 1048576 | tf_op jit(solution)/shard_map/all_to_all | solution.py:148
  167.0 39.9 %all-gather.2 = f32[64,2,128]{2,1,0:T(2,128)S(1)} all-gather(f32[1,2,128]{2,1,0:T(2,128)S(1)} %maximum_bitcast_fusion.3), channel_id=3, replica_groups=mesh['seq'=64,'tok'=8] {'seq'}, dimensions={0}, use_global_device_ids=true | all-gather | bytes 66560 | tf_op jit(solution)/shard_map/all_gather | solution.py:107
  206.9 4.3 %multiply_reduce_fusion.2 = f32[2,128,128]{2,1,0:T(8,128)S(1)} fusion(f32[64,2,128,128]{3,2,1,0:T(8,128)} %bitcast.171, f32[64]{0:T(128)S(1)} %compare_convert_fusion), kind=kLoop, calls=%fused_computation.50 | loop fusion | flops 4161536 | bytes 8519936 | tf_op jit(solution)/shard_map/reduce_sum | solution.py:110
  213.6 6.8 %all-to-all-start.6 = ((bf16[8,128,256]{1,2,0:T(8,128)(2,1)}), bf16[8,128,256]{1,2,0:T(8,128)(2,1)S(1)}, u32[]{:S(2)}, u32[]{:S(2)}) async-start(bf16[8,128,256]{1,2,0:T(8,128)(2,1)} %copy_bitcast_fusion.3), calls=%async_computation.6 | async-start | bytes 1048576 | tf_op jit(solution)/shard_map/all_to_all | solution.py:150
  220.6 1.0 copy.45
  221.9 1.5 fusion.44
  224.8 13.7 %all-to-all-done.6 = bf16[8,128,256]{1,2,0:T(8,128)(2,1)S(1)} async-done(((bf16[8,128,256]{1,2,0:T(8,128)(2,1)}), bf16[8,128,256]{1,2,0:T(8,128)(2,1)S(1)}, u32[]{:S(2)}, u32[]{:S(2)}) %all-to-all-start.6) | async-done | bytes 524320 | tf_op jit(solution)/shard_map/all_to_all | solution.py:150
  238.5 3.5 %all-to-all-start.5 = ((bf16[8,128,256]{1,2,0:T(8,128)(2,1)}), bf16[8,128,256]{1,2,0:T(8,128)(2,1)S(1)}, u32[]{:S(2)}, u32[]{:S(2)}) async-start(bf16[8,128,256]{1,2,0:T(8,128)(2,1)} %copy_bitcast_fusion.4), calls=%async_computation.5 | async-start | bytes 1048576 | tf_op jit(solution)/shard_map/all_to_all | solution.py:149
  242.0 1.0 copy.51
  243.0 1.0 copy.53
  244.0 15.9 %all-to-all-done.5 = bf16[8,128,256]{1,2,0:T(8,128)(2,1)S(1)} async-done(((bf16[8,128,256]{1,2,0:T(8,128)(2,1)}), bf16[8,128,256]{1,2,0:T(8,128)(2,1)S(1)}, u32[]{:S(2)}, u32[]{:S(2)}) %all-to-all-start.5) | async-done | bytes 524320 | tf_op jit(solution)/shard_map/all_to_all | solution.py:149
  259.9 1.0 copy.52
  (142 shorter events, 30.9 us)
Async XLA Ops:
  7.2 13.1 %copy-start.15 = (bf16[128,2048]{1,0:T(8,128)(2,1)S(1)}, bf16[128,2048]{1,0:T(8,128)(2,1)}, u32[]{:S(2)}) copy-start(bf16[128,2048]{1,0:T(8,128)(2,1)} %param.14) | copy-start | bytes 1572868
  7.2 34.6 %copy-start.27 = (f32[16]{0:T(128)S(1)}, f32[16]{0:T(128)}, u32[]{:S(2)}) copy-start(f32[16]{0:T(128)} %param.17) | copy-start | bytes 196
  9.3 33.3 %copy-start.25 = (f32[1,2,128]{2,1,0:T(2,128)S(1)}, f32[1,2,128]{2,1,0:T(2,128)}, u32[]{:S(2)}) copy-start(f32[1,2,128]{2,1,0:T(2,128)} %param.16) | copy-start | bytes 3076
  9.3 29.0 %all-to-all-start = ((bf16[128,8,256]{0,2,1:T(8,128)(2,1)}), bf16[128,8,256]{0,2,1:T(8,128)(2,1)S(1)}, u32[]{:S(2)}, u32[]{:S(2)}) async-start(bf16[128,8,256]{0,2,1:T(8,128)(2,1)} %bitcast), calls=%async_computation | async-start | bytes 1048576 | tf_op jit(solution)/shard_map/all_to_all | solution.py:75
  38.2 21.4 %all-to-all-start.2 = ((bf16[128,8,256]{0,2,1:T(8,128)(2,1)}), bf16[128,8,256]{0,2,1:T(8,128)(2,1)S(1)}, u32[]{:S(2)}, u32[]{:S(2)}) async-start(bf16[128,8,256]{0,2,1:T(8,128)(2,1)} %bitcast.5), calls=%async_computation.2 | async-start | bytes 1048576 | tf_op jit(solution)/shard_map/all_to_all | solution.py:78
  41.7 165.1 %all-gather.5.cloned.1.call-start = ((), (), s32[]{:S(2)}) async-start(), calls=%async_computation.7 | async-start | bytes 8519680 | tf_op jit(solution)/shard_map/all_gather | solution.py:106
  42.6 47.8 %copy-start.2 = (bf16[1024,256]{0,1:T(8,128)(2,1)}, bf16[1024,256]{0,1:T(8,128)(2,1)S(1)}, u32[]{:S(2)}) copy-start(bf16[1024,256]{0,1:T(8,128)(2,1)S(1)} %copy_bitcast_fusion.2) | copy-start | bytes 1572868
  59.7 31.5 %copy-start.8 = (bf16[1024,256]{0,1:T(8,128)(2,1)}, bf16[1024,256]{0,1:T(8,128)(2,1)S(1)}, u32[]{:S(2)}) copy-start(bf16[1024,256]{0,1:T(8,128)(2,1)S(1)} %copy_bitcast_fusion) | copy-start | bytes 1572868
  61.0 2.2 copy-start.16
  61.1 7.9 %copy-start.17 = (bf16[128,2048]{1,0:T(8,128)(2,1)S(1)}, bf16[128,2048]{1,0:T(8,128)(2,1)}, u32[]{:S(2)}) copy-start(bf16[128,2048]{1,0:T(8,128)(2,1)} %param.13) | copy-start | bytes 1572868
  64.2 21.4 %all-to-all-start.1 = ((bf16[128,8,256]{0,2,1:T(8,128)(2,1)}), bf16[128,8,256]{0,2,1:T(8,128)(2,1)S(1)}, u32[]{:S(2)}, u32[]{:S(2)}) async-start(bf16[128,8,256]{0,2,1:T(8,128)(2,1)} %bitcast.2), calls=%async_computation.1 | async-start | bytes 1048576 | tf_op jit(solution)/shard_map/all_to_all | solution.py:76
  85.6 20.1 %all-to-all-start.3 = ((bf16[128,8,256]{2,0,1:T(8,128)(2,1)}), bf16[128,8,256]{2,0,1:T(8,128)(2,1)S(1)}, u32[]{:S(2)}, u32[]{:S(2)}) async-start(bf16[128,8,256]{2,0,1:T(8,128)(2,1)} %bitcast.177), calls=%async_computation.3 | async-start | bytes 1048576 | tf_op jit(solution)/shard_map/all_to_all | solution.py:77
  89.3 0.9 copy-start.6
  105.7 1.7 copy-start.4
  110.7 2.5 copy-start.23
  110.7 2.5 copy-start.24
  114.3 1.0 copy-start.1
  114.9 1.1 copy-start.13
  116.4 0.8 copy-start.14
  120.5 2.7 %copy-start.23 = (bf16[1024,128]{0,1:T(8,128)(2,1)S(1)}, bf16[1024,128]{0,1:T(8,128)(2,1)}, u32[]{:S(2)}) copy-start(bf16[1024,128]{0,1:T(8,128)(2,1)} %get-tuple-element.504) | copy-start | bytes 786436 | tf_op jit(solution)/shard_map/while
  120.5 2.7 %copy-start.24 = (bf16[1024,128]{1,0:T(8,128)(2,1)S(1)}, bf16[1024,128]{1,0:T(8,128)(2,1)}, u32[]{:S(2)}) copy-start(bf16[1024,128]{1,0:T(8,128)(2,1)} %get-tuple-element.505) | copy-start | bytes 786436 | tf_op jit(solution)/shard_map/while
  124.3 1.0 copy-start.1
  124.9 1.1 copy-start.13
  126.4 0.8 copy-start.14
  134.6 2.5 copy-start.21
  134.7 2.5 copy-start.22
  138.2 1.0 copy-start
  138.9 1.1 copy-start.10
  140.4 0.8 copy-start.11
  144.5 2.7 %copy-start.21 = (bf16[1024,128]{0,1:T(8,128)(2,1)S(1)}, bf16[1024,128]{0,1:T(8,128)(2,1)}, u32[]{:S(2)}) copy-start(bf16[1024,128]{0,1:T(8,128)(2,1)} %get-tuple-element.462) | copy-start | bytes 786436 | tf_op jit(solution)/shard_map/while
  144.5 2.7 %copy-start.22 = (bf16[1024,128]{1,0:T(8,128)(2,1)S(1)}, bf16[1024,128]{1,0:T(8,128)(2,1)}, u32[]{:S(2)}) copy-start(bf16[1024,128]{1,0:T(8,128)(2,1)} %get-tuple-element.463) | copy-start | bytes 786436 | tf_op jit(solution)/shard_map/while
  148.3 1.0 copy-start
  148.9 1.1 copy-start.10
  150.4 0.8 copy-start.11
  151.2 3.4 %copy-start.12 = (f32[2,512,128]{2,1,0:T(8,128)S(1)}, f32[2,512,128]{2,1,0:T(8,128)}, u32[]{:S(2)}) copy-start(f32[2,512,128]{2,1,0:T(8,128)} %get-tuple-element.112) | copy-start | bytes 1572868
  151.2 4.4 %copy-start.3 = (bf16[1024,256]{0,1:T(8,128)(2,1)S(1)}, bf16[1024,256]{0,1:T(8,128)(2,1)}, u32[]{:S(2)}) copy-start(bf16[1024,256]{0,1:T(8,128)(2,1)} %copy-done.2) | copy-start | bytes 1572868
  151.2 4.4 %copy-start.9 = (bf16[1024,256]{0,1:T(8,128)(2,1)S(1)}, bf16[1024,256]{0,1:T(8,128)(2,1)}, u32[]{:S(2)}) copy-start(bf16[1024,256]{0,1:T(8,128)(2,1)} %copy-done.8) | copy-start | bytes 1572868
  151.2 4.4 %copy-start.26 = (f32[1,2,128,128]{3,2,1,0:T(8,128)S(1)}, f32[1,2,128,128]{3,2,1,0:T(8,128)}, u32[]{:S(2)}) copy-start(f32[1,2,128,128]{3,2,1,0:T(8,128)} %param.15) | copy-start | bytes 393220
  155.7 2.9 %copy-start.20 = (f32[1024,128]{0,1:T(8,128)S(1)}, f32[1024,128]{0,1:T(8,128)}, u32[]{:S(2)}) copy-start(f32[1024,128]{0,1:T(8,128)} %copy.54) | copy-start | bytes 1572868
  158.5 1.5 copy-start.19
  162.3 51.3 %all-to-all-start.4 = ((bf16[8,128,256]{1,2,0:T(8,128)(2,1)}), bf16[8,128,256]{1,2,0:T(8,128)(2,1)S(1)}, u32[]{:S(2)}, u32[]{:S(2)}) async-start(bf16[8,128,256]{1,2,0:T(8,128)(2,1)} %copy_bitcast_fusion.5), calls=%async_computation.4 | async-start | bytes 1048576 | tf_op jit(solution)/shard_map/all_to_all | solution.py:148
  206.9 4.4 %copy-start.7 = (bf16[1024,256]{0,1:T(8,128)(2,1)S(1)}, bf16[1024,256]{0,1:T(8,128)(2,1)}, u32[]{:S(2)}) copy-start(bf16[1024,256]{0,1:T(8,128)(2,1)} %copy-done.6) | copy-start | bytes 1572868
  206.9 4.4 %copy-start.18 = (f32[1024,128]{0,1:T(8,128)S(1)}, f32[1024,128]{0,1:T(8,128)}, u32[]{:S(2)}) copy-start(f32[1024,128]{0,1:T(8,128)} %copy.48) | copy-start | bytes 1572868
  212.7 9.1 %copy-start.5 = (bf16[128,8,256]{2,0,1:T(8,128)(2,1)S(1)}, bf16[128,8,256]{2,0,1:T(8,128)(2,1)}, u32[]{:S(2)}) copy-start(bf16[128,8,256]{2,0,1:T(8,128)(2,1)} %copy-done.4) | copy-start | bytes 1572868
  213.6 24.9 %all-to-all-start.6 = ((bf16[8,128,256]{1,2,0:T(8,128)(2,1)}), bf16[8,128,256]{1,2,0:T(8,128)(2,1)S(1)}, u32[]{:S(2)}, u32[]{:S(2)}) async-start(bf16[8,128,256]{1,2,0:T(8,128)(2,1)} %copy_bitcast_fusion.3), calls=%async_computation.6 | async-start | bytes 1048576 | tf_op jit(solution)/shard_map/all_to_all | solution.py:150
  238.5 21.4 %all-to-all-start.5 = ((bf16[8,128,256]{1,2,0:T(8,128)(2,1)}), bf16[8,128,256]{1,2,0:T(8,128)(2,1)S(1)}, u32[]{:S(2)}, u32[]{:S(2)}) async-start(bf16[8,128,256]{1,2,0:T(8,128)(2,1)} %copy_bitcast_fusion.4), calls=%async_computation.5 | async-start | bytes 1048576 | tf_op jit(solution)/shard_map/all_to_all | solution.py:149
Sparse Core Ops, SparseCore 0:
  63.3 84.5 all-gather.4
where the time goes:
time: 269 us; the launch traced here: 268 us
  waiting for transfers between devices  91.9 us (34%)
  blocking collectives  39.9 us (15%)
  matrix products  39.2 us (15%)
  starting transfers between devices  35.5 us (13%)
  local copies, waits for them, and re-layouts  30.3 us (11%)
  between operations  15.7 us (6%)
  other arithmetic  12.3 us (5%)
  loops' own time  2.88 us (1%)
    all_gather x1, blocking collectives, body(): lax.all_gather(normal_grads, 'seq', axis=0, tiled=True)  39.9 us
    all_to_all x1, waiting for transfers between devices, body(): lax.all_to_all(queries, 'tok', split_axis=1, concat_axis=0, tiled=True)  17 us
    all_to_all x1, waiting for transfers between devices, body(): lax.all_to_all(grad_output, 'tok', split_axis=1, concat_axis=0, tiled=True)  16 us
    all_to_all x1, waiting for transfers between devices, body(): lax.all_to_all(key_grads, 'tok', split_axis=0, concat_axis=1, tiled=True)  15.9 us
    all_to_all x1, waiting for transfers between devices, body(): lax.all_to_all(key_vectors, 'tok', split_axis=1, concat_axis=0, tiled=True)  15.7 us
    all_to_all x1, waiting for transfers between devices, body(): lax.all_to_all(value_grads, 'tok', split_axis=0, concat_axis=1, tiled=True)  13.7 us
    all_to_all x1, waiting for transfers between devices, body(): lax.all_to_all(value_vectors, 'tok', split_axis=1, concat_axis=0, tiled=T...  13.6 us
    all_to_all x1, starting transfers between devices, body(): lax.all_to_all(queries, 'tok', split_axis=1, concat_axis=0, tiled=True)  11 us
  transfers between devices with their start and end apart: 8, of which 6 were waited for; matrix products, arithmetic and copies ran while one was open for 26% of the time, Pallas kernels for 0%

commit v1 on v0

v1 whole, which is shorter than its diff:
```python
import functools

import jax
import jax.numpy as jnp
from jax import lax
from jax.experimental import pallas as pl
from jax.experimental.pallas import tpu as pltpu
from jax.sharding import PartitionSpec as P

SEQ_GRID = (8, 4)
LOG2E = 1.4426950408889634
VMEM_LIMIT = 48 * 1024 * 1024
F32 = jnp.float32
BF16 = jnp.bfloat16


def params():
    return pltpu.CompilerParams(vmem_limit_bytes=VMEM_LIMIT)


def cost(flops, moved):
    return pl.CostEstimate(flops=int(flops), bytes_accessed=int(moved), transcendentals=0)


def split(value):
    high = value.astype(BF16)
    return high, (value - high.astype(F32)).astype(BF16)


def dot(left, right, left_dim=1, right_dim=0):
    return lax.dot_general(
        left, right, (((left_dim,), (right_dim,)), ((), ())), preferred_element_type=F32
    )


def dot3(left, right, left_dim=1, right_dim=0):
    (lh, ll), (rh, rl) = left, right
    return (
        dot(lh, rh, left_dim, right_dim)
        + dot(lh, rl, left_dim, right_dim)
        + dot(ll, rh, left_dim, right_dim)
    )


def feature_map(inputs):
    lower = jnp.exp(jnp.minimum(inputs, 0.0))
    positive = inputs > 0
    return jnp.where(positive, inputs + 1.0, lower), jnp.where(positive, 1.0, lower)


def rows_of(block):
    return block.reshape(block.shape[0] * block.shape[1], block.shape[2])


def pack_kernel(count, *refs):
    sources, (target, sems) = refs[:count], refs[count:]
    groups, _, _, width = target.shape
    copies = []
    for group in range(groups):
        for which, source in enumerate(sources):
            copies.append(
                pltpu.make_async_copy(
                    source.at[:, pl.ds(group * width, width)],
                    target.at[group, which],
                    sems.at[group * count + which],
                )
            )
    for copy in copies:
        copy.start()
    for copy in copies:
        copy.wait()


def pack(arrays, groups):
    rows, columns = arrays[0].shape
    count = len(arrays)
    return pl.pallas_call(
        functools.partial(pack_kernel, count),
        out_shape=jax.ShapeDtypeStruct((groups, count, rows, columns // groups), arrays[0].dtype),
        in_specs=[pl.BlockSpec(memory_space=pl.ANY)] * count,
        out_specs=pl.BlockSpec(memory_space=pltpu.VMEM),
        scratch_shapes=[pltpu.SemaphoreType.DMA((groups * count,))],
        cost_estimate=cost(0, 4 * count * rows * columns),
        name="pack",
    )(*arrays)


def unpack_kernel(count, source, *refs):
    targets, sems = refs[:count], refs[count]
    groups, _, _, width = source.shape
    copies = []
    for group in range(groups):
        for which, target in enumerate(targets):
            copies.append(
                pltpu.make_async_copy(
                    source.at[group, which],
                    target.at[:, pl.ds(group * width, width)],
                    sems.at[group * count + which],
                )
            )
    for copy in copies:
        copy.start()
    for copy in copies:
        copy.wait()


def unpack(array):
    groups, count, rows, width = array.shape
    return pl.pallas_call(
        functools.partial(unpack_kernel, count),
        out_shape=[jax.ShapeDtypeStruct((rows, groups * width), array.dtype)] * count,
        in_specs=[pl.BlockSpec(array.shape, lambda: (0, 0, 0, 0))],
        out_specs=[pl.BlockSpec(memory_space=pl.ANY)] * count,
        scratch_shapes=[pltpu.SemaphoreType.DMA((groups * count,))],
        cost_estimate=cost(0, 4 * array.size),
        name="unpack",
    )(array)


def read_kernel(gate_ref, both_ref, memory_ref, normal_ref, sums_ref, part_ref):
    gate = gate_ref[pl.program_id(0)]
    query = rows_of(both_ref[:, 0]).astype(F32)
    grad = rows_of(both_ref[:, 1]).astype(F32)
    memory = memory_ref[0]
    normal = normal_ref[0]
    size = memory.shape[0]
    features, slopes = feature_map(query)
    features2 = split(features)
    memory2 = split(memory)
    numerator = dot3(features2, memory2)
    inverse = 1.0 / jnp.sum(features * normal, axis=1, keepdims=True)
    scaled = gate * grad
    grad_numerator = scaled * inverse
    grad_denominator = -jnp.sum(scaled * numerator, axis=1, keepdims=True) * inverse * inverse
    numerator2 = split(grad_numerator)
    sums_ref[0, :size, :] = dot3(features2, numerator2, 0, 0)
    normal_grad = jnp.sum(features * grad_denominator, axis=0, keepdims=True)
    sums_ref[0, size:, :] = jnp.broadcast_to(normal_grad, (8, size))
    part_ref[...] = (dot3(numerator2, memory2, 1, 1) + grad_denominator * normal) * slopes


def memory_read(gates, both, memory, normalizer):
    groups, _, rows, width = both.shape
    heads, size, _ = memory.shape
    return pl.pallas_call(
        read_kernel,
        grid=(heads,),
        out_shape=[
            jax.ShapeDtypeStruct((heads, size + 8, size), F32),
            jax.ShapeDtypeStruct((groups * rows, width), F32),
        ],
        in_specs=[
            pl.BlockSpec(memory_space=pltpu.SMEM),
            pl.BlockSpec((groups, 2, rows, size), lambda h: (0, 0, 0, h)),
            pl.BlockSpec((1, size, size), lambda h: (h, 0, 0)),
            pl.BlockSpec((1, 1, size), lambda h: (h, 0, 0)),
        ],
        out_specs=[
            pl.BlockSpec((1, size + 8, size), lambda h: (h, 0, 0)),
            pl.BlockSpec((groups * rows, size), lambda h: (0, h)),
        ],
        compiler_params=params(),
        cost_estimate=cost(heads * 9 * 2 * groups * rows * size * size * 2, 4e6),
        name="memory_read",
    )(gates, both, memory, normalizer)


def attend_kernel(block, head, gate_ref, qo_ref, kv_ref, part_ref, dq_ref, dk_ref, dv_ref):
    local_share = 1.0 - gate_ref[head]
    query = rows_of(qo_ref[:, 0])
    grad = rows_of(qo_ref[:, 1])
    key = rows_of(kv_ref[:, 0])
    value = rows_of(kv_ref[:, 1])
    total, size = query.shape
    scale = size**-0.5
    for start in range(0, total, block):
        count = start + block
        q = query[start:count]
        o = grad[start:count]
        k = key[:count]
        scores = dot(k, q, 1, 1)
        diagonal = scores[start:]
        keep = lax.broadcasted_iota(jnp.int32, diagonal.shape, 0) <= lax.broadcasted_iota(
            jnp.int32, diagonal.shape, 1
        )
        diagonal = jnp.where(keep, diagonal, -1e30)
        scores = jnp.concatenate([scores[:start], diagonal], axis=0) if start else diagonal
        highest = jnp.max(scores, axis=0, keepdims=True)
        factor = scale * LOG2E
        weights = jnp.exp2(scores * factor - highest * factor)
        inverse = 1.0 / jnp.sum(weights, axis=0, keepdims=True)
        moved = dot(value[:count], o, 1, 1)
        centre = jnp.sum(weights * moved, axis=0, keepdims=True) * inverse
        attention = (weights * inverse).astype(BF16)
        grad_scores = (weights * (inverse * local_share) * (moved - centre)).astype(BF16)
        grad_query = dot(grad_scores, k, 0, 0)
        dq_ref[start:count, :] = (scale * grad_query + part_ref[start:count, :]).astype(BF16)
        grad_key = scale * dot(grad_scores, q)
        grad_value = local_share * dot(attention, o)
        if start:
            dk_ref[:start, :] += grad_key[:start]
            dv_ref[:start, :] += grad_value[:start]
        dk_ref[start:count, :] = grad_key[start:]
        dv_ref[start:count, :] = grad_value[start:]


def attend(head, gates, qo, kv, part):
    groups, _, rows, width = qo.shape
    total = groups * rows
    size = width // gates.shape[0]
    four = pl.BlockSpec((groups, 2, rows, size), lambda i: (0, 0, 0, head))
    flat = pl.BlockSpec((total, size), lambda i: (0, 0))
    return pl.pallas_call(
        functools.partial(attend_kernel, min(256, total), head),
        grid=(1,),
        out_shape=[
            jax.ShapeDtypeStruct((total, size), BF16),
            jax.ShapeDtypeStruct((total, size), F32),
            jax.ShapeDtypeStruct((total, size), F32),
        ],
        in_specs=[
            pl.BlockSpec(memory_space=pltpu.SMEM),
            four,
            four,
            pl.BlockSpec((total, size), lambda i: (0, head)),
        ],
        out_specs=[flat, flat, flat],
        compiler_params=params(),
        cost_estimate=cost(16 * total * total * size, 4e6),
        name="attend",
    )(gates, qo, kv, part)


def write_kernel(kv_ref, later_ref, *refs):
    heads, padded, size = later_ref.shape
    parts, out_ref = refs[:-1], refs[-1]
    groups, _, rows, _ = out_ref.shape
    for head in range(heads):
        columns = pl.ds(head * size, size)
        dq_ref, dk_ref, dv_ref = parts[3 * head : 3 * head + 3]
        key = rows_of(kv_ref[:, 0, :, columns]).astype(F32)
        value = rows_of(kv_ref[:, 1, :, columns])
        later = split(later_ref[head, :size, :])
        later_normal = later_ref[head, size : size + 1, :]
        features, slopes = feature_map(key)
        high, low = later
        grad_features = dot(value, high, 1, 1) + dot(value, low, 1, 1) + later_normal
        grad_key = dk_ref[...] + grad_features * slopes
        grad_value = dv_ref[...] + dot3(split(features), later)
        out_ref[:, 0, :, columns] = dq_ref[...].reshape(groups, rows, size)
        out_ref[:, 1, :, columns] = grad_key.astype(BF16).reshape(groups, rows, size)
        out_ref[:, 2, :, columns] = grad_value.astype(BF16).reshape(groups, rows, size)


def memory_write(kv, later, parts):
    groups, _, rows, width = kv.shape
    heads, padded, size = later.shape
    return pl.pallas_call(
        write_kernel,
        out_shape=jax.ShapeDtypeStruct((groups, 3, rows, width), BF16),
        compiler_params=params(),
        cost_estimate=cost(heads * 5 * 2 * groups * rows * size * size * 2, 4e6),
        name="memory_write",
    )(kv, later, *parts)


def later_sums(sums, rows, columns):
    me = lax.axis_index("seq")
    second = me % 2 == 1
    line = 2 * columns

    def send(value, pairs):
        return lax.ppermute(value, "seq", pairs)

    def swap(value):
        return send(value, [(i, i ^ 1) for i in range(rows * line)])

    mine = jnp.where(second, sums[1], sums[0])
    other = jnp.where(second, sums[0], sums[1])
    received = swap(other)
    chip = mine + received
    below = None
    step = 1
    while step < rows:
        sent = chip if below is None else chip + below
        got = send(sent, [(i, i - step * line) for i in range(step * line, rows * line)])
        below = got if below is None else below + got
        step *= 2
    column = (me // 2) % columns
    whole = chip + below
    later = below
    for shift in range(1, columns):
        value = jnp.where(column >= shift, whole, below)
        pairs = [
            ((r * columns + c) * 2 + k, (r * columns + (c - shift) % columns) * 2 + k)
            for r in range(rows)
            for c in range(columns)
            for k in range(2)
        ]
        later = later + send(value, pairs)
    returned = swap(jnp.where(second, later + mine, later))
    kept = jnp.where(second, later, later + received)
    return jnp.where(second, jnp.stack([returned, kept]), jnp.stack([kept, returned]))


def exchange(array):
    return lax.all_to_all(array, "tok", split_axis=0, concat_axis=0, tiled=True)


def body(queries, key_vectors, value_vectors, grad_output, memory, normalizer, gate_logit):
    groups = lax.axis_size("tok")
    heads = gate_logit.shape[0] // groups
    gates = jax.nn.sigmoid(
        lax.dynamic_slice_in_dim(gate_logit, lax.axis_index("tok") * heads, heads)
    )
    qo = exchange(pack([queries, grad_output], groups))
    kv = exchange(pack([key_vectors, value_vectors], groups))
    sums, part = memory_read(gates, qo, memory[0], normalizer[0][:, None, :])
    later = later_sums(sums, *SEQ_GRID)
    parts = [value for head in range(heads) for value in attend(head, gates, qo, kv, part)]
    return tuple(unpack(exchange(memory_write(kv, later, parts))))


def solution(mesh):
    in_specs = (
        P(("seq", "tok"), None),
        P(("seq", "tok"), None),
        P(("seq", "tok"), None),
        P(("seq", "tok"), None),
        P("seq", "tok", None, None),
        P("seq", "tok", None),
        P(),
    )
    out_specs = (P(("seq", "tok"), None), P(("seq", "tok"), None), P(("seq", "tok"), None))
    return jax.shard_map(body, mesh=mesh, in_specs=in_specs, out_specs=out_specs, check_vma=False)
```

time: 269 us -> 151 us (0.56)
  waiting for transfers between devices: 91.9 us -> 45.7 us
  matrix products: 39.2 us -> 0 us
  local copies, waits for them, and re-layouts: 30.3 us -> 0.02 us
  Pallas kernels: 0 us -> 18.3 us
  between operations: 15.7 us -> 0.91 us
  other arithmetic: 12.3 us -> 2.38 us
  blocking collectives: 39.9 us -> 45.6 us
  loops' own time: 2.88 us -> 0 us
    all_to_all x7 -> x2, waiting for transfers between devices: 91.9 us -> 34.8 us  [exchange(): return lax.all_to_all(array, 'tok', split_axis=0, concat_axis=0, tiled=True)]
    all_to_all x0 -> x1, blocking collectives: none -> 45.6 us  [exchange(): return lax.all_to_all(array, 'tok', split_axis=0, concat_axis=0, tiled=True)]
    all_gather x1 -> x0, blocking collectives: 39.9 us -> none  [body(): lax.all_gather(normal_grads, 'seq', axis=0, tiled=True)]
    dot_general x34 -> x0, matrix products: 39.2 us -> none  [the longest x4 10.3 us: attend_rows(): jnp.einsum('qk,qd->kd', attention.astype(jnp.bfloat16), grad_rows, prefer...]
    all_to_all x7 -> x2, starting transfers between devices: 35.5 us -> 14.4 us  [exchange(): return lax.all_to_all(array, 'tok', split_axis=0, concat_axis=0, tiled=True)]
    ppermute x0 -> x8, starting transfers between devices: none -> 20.6 us  [send(): return lax.ppermute(value, 'seq', pairs)]
    pallas_call x0 -> x7, Pallas kernels: none -> 18.3 us  [the longest x2 7.5 us: attend(): pl.pallas_call(functools.partial(attend_kernel, min(256, total), head), g...]
    ppermute x0 -> x8, waiting for transfers between devices: none -> 10.9 us  [send(): return lax.ppermute(value, 'seq', pairs)]
  transfers between devices with their start and end apart: 8 -> 10, of which waited for: 6 -> 6; matrix products, arithmetic and copies ran while one was open for 26% -> 2% of each run, Pallas kernels for 0% -> 8%
where the time goes in v1:
time: 151 us; the launch traced here: 148 us
  waiting for transfers between devices  45.7 us (30%)
  blocking collectives  45.6 us (30%)
  starting transfers between devices  35.1 us (23%)
  Pallas kernels  18.3 us (12%)
  other arithmetic  2.38 us (2%)
    all_to_all x1, blocking collectives, exchange(): return lax.all_to_all(array, 'tok', split_axis=0, concat_axis=0, tiled=True)  45.6 us
    all_to_all x2, waiting for transfers between devices, exchange(): return lax.all_to_all(array, 'tok', split_axis=0, concat_axis=0, tiled=True)  34.8 us
    ppermute x8, starting transfers between devices, send(): return lax.ppermute(value, 'seq', pairs)  20.6 us
    all_to_all x2, starting transfers between devices, exchange(): return lax.all_to_all(array, 'tok', split_axis=0, concat_axis=0, tiled=True)  14.4 us
    ppermute x8, waiting for transfers between devices, send(): return lax.ppermute(value, 'seq', pairs)  10.9 us
    pallas_call x2, Pallas kernels, attend(): pl.pallas_call(functools.partial(attend_kernel, min(256, total), head), g...  7.5 us
    pallas_call x2, Pallas kernels, pack(): pl.pallas_call(functools.partial(pack_kernel, count), out_shape=jax.Shape...  4.75 us
  transfers between devices with their start and end apart: 10, of which 6 were waited for; matrix products, arithmetic and copies ran while one was open for 2% of the time, Pallas kernels for 8%

profile of v1, /device:TPU:1, one launch (start us, length us, event | category | flops | bytes accessed | tf_op | source)
XLA Modules:
  0.0 148.0 jit_solution(14957625776367298391)
XLA Ops:
  0.6 2.4 %pack.3 = bf16[8,2,128,256]{3,2,1,0:T(8,128)(2,1)} custom-call(bf16[128,2048]{1,0:T(8,128)(2,1)} %refs_0_.3, bf16[128,2048]{1,0:T(8,128)(2,1)} %refs_1_.3), custom_call_target="tpu_custom_call" | custom-call | bytes 2097152 | tf_op jit(solution)/shard_map/pack/pallas_call | solution.py:77
  3.0 10.9 %all-to-all-start.1 = ((bf16[8,2,128,256]{3,2,1,0:T(8,128)(2,1)}), bf16[8,2,128,256]{3,2,1,0:T(8,128)(2,1)S(1)}, u32[]{:S(2)}, u32[]{:S(2)}) async-start(bf16[8,2,128,256]{3,2,1,0:T(8,128)(2,1)} %pack.3), calls=%async_computation.1 | async-start | bytes 2097152 | tf_op jit(solution)/shard_map/all_to_all | solution.py:307
  13.9 2.4 %pack.2 = bf16[8,2,128,256]{3,2,1,0:T(8,128)(2,1)} custom-call(bf16[128,2048]{1,0:T(8,128)(2,1)} %refs_0_.2, bf16[128,2048]{1,0:T(8,128)(2,1)} %refs_1_.2), custom_call_target="tpu_custom_call" | custom-call | bytes 2097152 | tf_op jit(solution)/shard_map/pack/pallas_call | solution.py:77
  16.3 0.0 copy-start.3
  16.3 0.0 copy-start
  16.3 0.0 copy-start.1
  16.3 26.8 %all-to-all-done.1.both_ref.qo_ref = bf16[8,2,128,256]{3,2,1,0:T(8,128)(2,1)S(1)} async-done(((bf16[8,2,128,256]{3,2,1,0:T(8,128)(2,1)}), bf16[8,2,128,256]{3,2,1,0:T(8,128)(2,1)S(1)}, u32[]{:S(2)}, u32[]{:S(2)}) %all-to-all-start.1) | async-done | bytes 1048608 | tf_op jit(solution)/shard_map/all_to_all | solution.py:307
  43.1 3.6 %all-to-all-start = ((bf16[8,2,128,256]{3,2,1,0:T(8,128)(2,1)}), bf16[8,2,128,256]{3,2,1,0:T(8,128)(2,1)S(1)}, u32[]{:S(2)}, u32[]{:S(2)}) async-start(bf16[8,2,128,256]{3,2,1,0:T(8,128)(2,1)} %pack.2), calls=%async_computation | async-start | bytes 2097152 | tf_op jit(solution)/shard_map/all_to_all | solution.py:307
  46.6 0.0 copy-done.3
  46.7 0.1 add_divide_fusion.gate_ref
  46.7 0.0 copy-done
  46.7 0.0 copy-done.1
  46.7 2.4 %memory_read.1 = (f32[2,136,128]{2,1,0:T(8,128)S(1)}, f32[1024,256]{1,0:T(8,128)S(1)}) custom-call(f32[2]{0:T(128)S(1)} %add_divide_fusion.gate_ref, bf16[8,2,128,256]{3,2,1,0:T(8,128)(2,1)S(1)} %all-to-all-done.1.both_ref.qo_ref, f32[2,128,128]{2,1,0:T(8,128)S(1)} %bitcast.10, f32[2,1,128]{2,1,0:T(1,128)S(1)} %bitcast.11), custom_call_target="tpu_custom_call" | custom-call | flops 1207959552 | bytes 4000000 | tf_op jit(solution)/shard_map/memory_read/pallas_call | solution.py:145
  49.1 2.4 %collective-permute-start = (f32[136,128]{1,0:T(8,128)S(1)}, f32[136,128]{1,0:T(8,128)S(1)}, u32[]{:S(2)}, u32[]{:S(2)}) collective-permute-start(f32[136,128]{1,0:T(8,128)S(1)} %select_bitcast_fusion), channel_id=1, source_target_pairs={{0,8},{8,0},{16,24},{24,16},{32,40},{40,32},{48,56},{56,48},{64,72... | collective-permute-start | bytes 208904 | tf_op jit(solution)/shard_map/ppermute | solution.py:273
  51.6 0.9 collective-permute-done
  52.5 1.3 collective-permute-start.1
  53.8 4.0 %collective-permute-done.1 = f32[136,128]{1,0:T(8,128)S(1)} collective-permute-done((f32[136,128]{1,0:T(8,128)S(1)}, f32[136,128]{1,0:T(8,128)S(1)}, u32[]{:S(2)}, u32[]{:S(2)}) %collective-permute-start.1) | collective-permute-done | bytes 69664 | tf_op jit(solution)/shard_map/ppermute | solution.py:273
  57.8 0.6 add.51
  58.5 1.3 collective-permute-start.2
  59.8 5.1 %collective-permute-done.2 = f32[136,128]{1,0:T(8,128)} collective-permute-done((f32[136,128]{1,0:T(8,128)}, f32[136,128]{1,0:T(8,128)}, u32[]{:S(2)}, u32[]{:S(2)}) %collective-permute-start.2) | collective-permute-done | bytes 69664 | tf_op jit(solution)/shard_map/ppermute | solution.py:273
  64.9 1.5 %fusion.1 = (f32[136,128]{1,0:T(8,128)}, f32[136,128]{1,0:T(8,128)}) fusion(f32[136,128]{1,0:T(8,128)S(1)} %bitcast_add_fusion, f32[136,128]{1,0:T(8,128)S(1)} %collective-permute-done.1, f32[136,128]{1,0:T(8,128)} %collective-permute-done.2), kind=kLoop, calls=%fused_computation.12 | loop fusion | flops 34816 | bytes 348160 | tf_op jit(solution)/shard_map/add | solution.py:285
  66.4 1.3 collective-permute-start.3
  67.7 8.1 %all-to-all-done.kv_ref = bf16[8,2,128,256]{3,2,1,0:T(8,128)(2,1)S(1)} async-done(((bf16[8,2,128,256]{3,2,1,0:T(8,128)(2,1)}), bf16[8,2,128,256]{3,2,1,0:T(8,128)(2,1)S(1)}, u32[]{:S(2)}, u32[]{:S(2)}) %all-to-all-start) | async-done | bytes 1048608 | tf_op jit(solution)/shard_map/all_to_all | solution.py:307
  75.8 0.0 copy-start.2
  75.8 3.8 %attend.2 = (bf16[1024,128]{1,0:T(8,128)(2,1)S(1)}, f32[1024,128]{1,0:T(8,128)S(1)}, f32[1024,128]{1,0:T(8,128)S(1)}) custom-call(f32[2]{0:T(128)S(1)} %add_divide_fusion.gate_ref, bf16[8,2,128,256]{3,2,1,0:T(8,128)(2,1)S(1)} %all-to-all-done.1.both_ref.qo_ref, bf16[8,2,128,256]{3,2,1,0:T(8,128)(2,1)S(1)} %all-to-all-done.kv_ref, ...), custom_call_target="tpu_custom_call" | custom-call | flops 2147483648 | bytes 4000000 | tf_op jit(solution)/shard_map/attend/pallas_call | solution.py:213
  79.5 0.0 collective-permute-done.3
  79.6 0.0 copy-done.2
  79.6 4.6 %collective-permute-start.5 = (f32[136,128]{1,0:T(8,128)S(1)}, f32[136,128]{1,0:T(8,128)S(1)}, u32[]{:S(2)}, u32[]{:S(2)}) collective-permute-start(f32[136,128]{1,0:T(8,128)S(1)} %get-tuple-element.25), channel_id=1, source_target_pairs={{0,32},{8,40},{16,48},{24,56},{32,0},{40,8},{48,16},{56,24},{64,96... | collective-permute-start | bytes 208904 | tf_op jit(solution)/shard_map/ppermute | solution.py:273
  84.3 2.2 %collective-permute-start.6 = (f32[136,128]{1,0:T(8,128)S(1)}, f32[136,128]{1,0:T(8,128)S(1)}, u32[]{:S(2)}, u32[]{:S(2)}) collective-permute-start(f32[136,128]{1,0:T(8,128)S(1)} %get-tuple-element.26), channel_id=1, source_target_pairs={{0,16},{8,24},{16,32},{24,40},{32,48},{40,56},{48,0},{56,8},{64,80... | collective-permute-start | bytes 208904 | tf_op jit(solution)/shard_map/ppermute | solution.py:273
  86.5 4.3 %collective-permute-start.4 = (f32[136,128]{1,0:T(8,128)S(1)}, f32[136,128]{1,0:T(8,128)S(1)}, u32[]{:S(2)}, u32[]{:S(2)}) collective-permute-start(f32[136,128]{1,0:T(8,128)S(1)} %get-tuple-element.21), channel_id=1, source_target_pairs={{0,48},{8,56},{16,0},{24,8},{32,16},{40,24},{48,32},{56,40},{64,11... | collective-permute-start | bytes 208904 | tf_op jit(solution)/shard_map/ppermute | solution.py:273
  90.8 3.7 %attend.3 = (bf16[1024,128]{1,0:T(8,128)(2,1)S(1)}, f32[1024,128]{1,0:T(8,128)S(1)}, f32[1024,128]{1,0:T(8,128)S(1)}) custom-call(f32[2]{0:T(128)S(1)} %add_divide_fusion.gate_ref, bf16[8,2,128,256]{3,2,1,0:T(8,128)(2,1)S(1)} %all-to-all-done.1.both_ref.qo_ref, bf16[8,2,128,256]{3,2,1,0:T(8,128)(2,1)S(1)} %all-to-all-done.kv_ref, ...), custom_call_target="tpu_custom_call" | custom-call | flops 2147483648 | bytes 4000000 | tf_op jit(solution)/shard_map/attend/pallas_call | solution.py:213
  94.5 0.0 collective-permute-done.5
  94.5 0.0 collective-permute-done.6
  94.6 0.0 collective-permute-done.4
  94.6 3.2 %collective-permute-start.7 = (f32[136,128]{1,0:T(8,128)S(1)}, f32[136,128]{1,0:T(8,128)S(1)}, u32[]{:S(2)}, u32[]{:S(2)}) collective-permute-start(f32[136,128]{1,0:T(8,128)S(1)} %get-tuple-element.19), channel_id=1, source_target_pairs={{0,8},{8,0},{16,24},{24,16},{32,40},{40,32},{48,56},{56,48},{64,72... | collective-permute-start | bytes 208904 | tf_op jit(solution)/shard_map/ppermute | solution.py:273
  97.9 0.9 collective-permute-done.7
  98.8 0.9 memory_write.1
  99.7 45.6 %all_to_all.15.source = bf16[8,3,128,256]{3,2,1,0:T(8,128)(2,1)} all-to-all(bf16[8,3,128,256]{3,2,1,0:T(8,128)(2,1)S(1)} %memory_write.1), channel_id=1, replica_groups=mesh['seq'=64,'tok'=8] {'tok'}, dimensions={0} | all-to-all | bytes 3145728 | tf_op jit(solution)/shard_map/all_to_all | solution.py:307
  145.3 2.7 %unpack.1 = (bf16[128,2048]{1,0:T(8,128)(2,1)}, bf16[128,2048]{1,0:T(8,128)(2,1)}, bf16[128,2048]{1,0:T(8,128)(2,1)}) custom-call(bf16[8,3,128,256]{3,2,1,0:T(8,128)(2,1)} %all_to_all.15.source), custom_call_target="tpu_custom_call" | custom-call | bytes 3145728 | tf_op jit(solution)/shard_map/unpack/pallas_call | solution.py:109
  (7 shorter events, 0.1 us)
Async XLA Ops:
  3.0 40.1 %all-to-all-start.1 = ((bf16[8,2,128,256]{3,2,1,0:T(8,128)(2,1)}), bf16[8,2,128,256]{3,2,1,0:T(8,128)(2,1)S(1)}, u32[]{:S(2)}, u32[]{:S(2)}) async-start(bf16[8,2,128,256]{3,2,1,0:T(8,128)(2,1)} %pack.3), calls=%async_computation.1 | async-start | bytes 2097152 | tf_op jit(solution)/shard_map/all_to_all | solution.py:307
  16.3 30.4 %copy-start.3 = (f32[16]{0:T(128)S(1)}, f32[16]{0:T(128)}, u32[]{:S(2)}) copy-start(f32[16]{0:T(128)} %param.13) | copy-start | bytes 196
  16.3 30.5 %copy-start = (f32[1,2,128,128]{3,2,1,0:T(8,128)S(1)}, f32[1,2,128,128]{3,2,1,0:T(8,128)}, u32[]{:S(2)}) copy-start(f32[1,2,128,128]{3,2,1,0:T(8,128)} %param.11) | copy-start | bytes 393220
  16.3 30.4 %copy-start.1 = (f32[1,2,128]{2,1,0:T(2,128)S(1)}, f32[1,2,128]{2,1,0:T(2,128)}, u32[]{:S(2)}) copy-start(f32[1,2,128]{2,1,0:T(2,128)} %param.12) | copy-start | bytes 3076
  43.1 32.7 %all-to-all-start = ((bf16[8,2,128,256]{3,2,1,0:T(8,128)(2,1)}), bf16[8,2,128,256]{3,2,1,0:T(8,128)(2,1)S(1)}, u32[]{:S(2)}, u32[]{:S(2)}) async-start(bf16[8,2,128,256]{3,2,1,0:T(8,128)(2,1)} %pack.2), calls=%async_computation | async-start | bytes 2097152 | tf_op jit(solution)/shard_map/all_to_all | solution.py:307
  49.1 3.3 %collective-permute-start = (f32[136,128]{1,0:T(8,128)S(1)}, f32[136,128]{1,0:T(8,128)S(1)}, u32[]{:S(2)}, u32[]{:S(2)}) collective-permute-start(f32[136,128]{1,0:T(8,128)S(1)} %select_bitcast_fusion), channel_id=1, source_target_pairs={{0,8},{8,0},{16,24},{24,16},{32,40},{40,32},{48,56},{56,48},{64,72... | collective-permute-start | bytes 208904 | tf_op jit(solution)/shard_map/ppermute | solution.py:273
  52.5 5.3 %collective-permute-start.1 = (f32[136,128]{1,0:T(8,128)S(1)}, f32[136,128]{1,0:T(8,128)S(1)}, u32[]{:S(2)}, u32[]{:S(2)}) collective-permute-start(f32[136,128]{1,0:T(8,128)S(1)} %bitcast_add_fusion), channel_id=1, source_target_pairs={{64,0},{72,8},{80,16},{88,24},{96,32},{104,40},{112,48},{120,56},{... | collective-permute-start | bytes 208904 | tf_op jit(solution)/shard_map/ppermute | solution.py:273
  58.5 6.4 %collective-permute-start.2 = (f32[136,128]{1,0:T(8,128)}, f32[136,128]{1,0:T(8,128)}, u32[]{:S(2)}, u32[]{:S(2)}) collective-permute-start(f32[136,128]{1,0:T(8,128)} %add.51), channel_id=1, source_target_pairs={{128,0},{136,8},{144,16},{152,24},{160,32},{168,40},{176,48},{184,... | collective-permute-start | bytes 208904 | tf_op jit(solution)/shard_map/ppermute | solution.py:273
  66.4 13.1 %collective-permute-start.3 = (f32[136,128]{1,0:T(8,128)}, f32[136,128]{1,0:T(8,128)S(1)}, u32[]{:S(2)}, u32[]{:S(2)}) collective-permute-start(f32[136,128]{1,0:T(8,128)} %get-tuple-element.23), channel_id=1, source_target_pairs={{256,0},{264,8},{272,16},{280,24},{288,32},{296,40},{304,48},{312,... | collective-permute-start | bytes 208904 | tf_op jit(solution)/shard_map/ppermute | solution.py:273
  75.8 3.8 %copy-start.2 = (f32[136,128]{1,0:T(8,128)S(1)}, f32[136,128]{1,0:T(8,128)}, u32[]{:S(2)}) copy-start(f32[136,128]{1,0:T(8,128)} %get-tuple-element.24) | copy-start | bytes 208900
  79.6 14.9 %collective-permute-start.5 = (f32[136,128]{1,0:T(8,128)S(1)}, f32[136,128]{1,0:T(8,128)S(1)}, u32[]{:S(2)}, u32[]{:S(2)}) collective-permute-start(f32[136,128]{1,0:T(8,128)S(1)} %get-tuple-element.25), channel_id=1, source_target_pairs={{0,32},{8,40},{16,48},{24,56},{32,0},{40,8},{48,16},{56,24},{64,96... | collective-permute-start | bytes 208904 | tf_op jit(solution)/shard_map/ppermute | solution.py:273
  84.3 10.3 %collective-permute-start.6 = (f32[136,128]{1,0:T(8,128)S(1)}, f32[136,128]{1,0:T(8,128)S(1)}, u32[]{:S(2)}, u32[]{:S(2)}) collective-permute-start(f32[136,128]{1,0:T(8,128)S(1)} %get-tuple-element.26), channel_id=1, source_target_pairs={{0,16},{8,24},{16,32},{24,40},{32,48},{40,56},{48,0},{56,8},{64,80... | collective-permute-start | bytes 208904 | tf_op jit(solution)/shard_map/ppermute | solution.py:273
  86.5 8.1 %collective-permute-start.4 = (f32[136,128]{1,0:T(8,128)S(1)}, f32[136,128]{1,0:T(8,128)S(1)}, u32[]{:S(2)}, u32[]{:S(2)}) collective-permute-start(f32[136,128]{1,0:T(8,128)S(1)} %get-tuple-element.21), channel_id=1, source_target_pairs={{0,48},{8,56},{16,0},{24,8},{32,16},{40,24},{48,32},{56,40},{64,11... | collective-permute-start | bytes 208904 | tf_op jit(solution)/shard_map/ppermute | solution.py:273
  94.6 4.1 %collective-permute-start.7 = (f32[136,128]{1,0:T(8,128)S(1)}, f32[136,128]{1,0:T(8,128)S(1)}, u32[]{:S(2)}, u32[]{:S(2)}) collective-permute-start(f32[136,128]{1,0:T(8,128)S(1)} %get-tuple-element.19), channel_id=1, source_target_pairs={{0,8},{8,0},{16,24},{24,16},{32,40},{40,32},{48,56},{56,48},{64,72... | collective-permute-start | bytes 208904 | tf_op jit(solution)/shard_map/ppermute | solution.py:273

commit v2 on v1

--- a/solution.py
+++ b/solution.py
@@ -9,7 +9,7 @@
 
 SEQ_GRID = (8, 4)
 LOG2E = 1.4426950408889634
-VMEM_LIMIT = 48 * 1024 * 1024
+VMEM_LIMIT = 24 * 1024 * 1024
 F32 = jnp.float32
 BF16 = jnp.bfloat16
 
@@ -46,6 +46,12 @@
     lower = jnp.exp(jnp.minimum(inputs, 0.0))
     positive = inputs > 0
     return jnp.where(positive, inputs + 1.0, lower), jnp.where(positive, 1.0, lower)
+
+
+def gate_of(gates_ref, head):
+    gates = gates_ref[...]
+    at = lax.broadcasted_iota(jnp.int32, gates.shape, 1) == head
+    return jnp.sum(jnp.where(at, gates, 0.0), axis=1, keepdims=True)
 
 
 def rows_of(block):
@@ -117,8 +123,8 @@
     )(array)
 
 
-def read_kernel(gate_ref, both_ref, memory_ref, normal_ref, sums_ref, part_ref):
-    gate = gate_ref[pl.program_id(0)]
+def read_kernel(gates_ref, both_ref, memory_ref, normal_ref, sums_ref, part_ref):
+    gate = gate_of(gates_ref, pl.program_id(0))
     query = rows_of(both_ref[:, 0]).astype(F32)
     grad = rows_of(both_ref[:, 1]).astype(F32)
     memory = memory_ref[0]
@@ -150,7 +156,7 @@
             jax.ShapeDtypeStruct((groups * rows, width), F32),
         ],
         in_specs=[
-            pl.BlockSpec(memory_space=pltpu.SMEM),
+            pl.BlockSpec(gates.shape, lambda i: (0, 0)),
             pl.BlockSpec((groups, 2, rows, size), lambda h: (0, 0, 0, h)),
             pl.BlockSpec((1, size, size), lambda h: (h, 0, 0)),
             pl.BlockSpec((1, 1, size), lambda h: (h, 0, 0)),
@@ -165,8 +171,8 @@
     )(gates, both, memory, normalizer)
 
 
-def attend_kernel(block, head, gate_ref, qo_ref, kv_ref, part_ref, dq_ref, dk_ref, dv_ref):
-    local_share = 1.0 - gate_ref[head]
+def attend_kernel(block, head, gates_ref, qo_ref, kv_ref, part_ref, dq_ref, dk_ref, dv_ref):
+    local_share = 1.0 - gate_of(gates_ref, head)
     query = rows_of(qo_ref[:, 0])
     grad = rows_of(qo_ref[:, 1])
     key = rows_of(kv_ref[:, 0])
@@ -207,7 +213,7 @@
 def attend(head, gates, qo, kv, part):
     groups, _, rows, width = qo.shape
     total = groups * rows
-    size = width // gates.shape[0]
+    size = width // gates.shape[1]
     four = pl.BlockSpec((groups, 2, rows, size), lambda i: (0, 0, 0, head))
     flat = pl.BlockSpec((total, size), lambda i: (0, 0))
     return pl.pallas_call(
@@ -219,7 +225,7 @@
             jax.ShapeDtypeStruct((total, size), F32),
         ],
         in_specs=[
-            pl.BlockSpec(memory_space=pltpu.SMEM),
+            pl.BlockSpec(gates.shape, lambda i: (0, 0)),
             four,
             four,
             pl.BlockSpec((total, size), lambda i: (0, head)),
@@ -312,7 +318,7 @@
     heads = gate_logit.shape[0] // groups
     gates = jax.nn.sigmoid(
         lax.dynamic_slice_in_dim(gate_logit, lax.axis_index("tok") * heads, heads)
-    )
+    )[None, :]
     qo = exchange(pack([queries, grad_output], groups))
     kv = exchange(pack([key_vectors, value_vectors], groups))
     sums, part = memory_read(gates, qo, memory[0], normalizer[0][:, None, :])

time: 151 us -> 150 us (level)
  transfers between devices with their start and end apart: 10 -> 10, of which waited for: 6 -> 6; matrix products, arithmetic and copies ran while one was open for 2% -> 2% of each run, Pallas kernels for 8% -> 7%
where the time goes in v2:
time: 150 us; the launch traced here: 147 us
  waiting for transfers between devices  46.2 us (31%)
  blocking collectives  45.6 us (30%)
  starting transfers between devices  35.1 us (23%)
  Pallas kernels  16.9 us (11%)
  other arithmetic  2.38 us (2%)
    all_to_all x1, blocking collectives, exchange(): return lax.all_to_all(array, 'tok', split_axis=0, concat_axis=0, tiled=True)  45.6 us
    all_to_all x2, waiting for transfers between devices, exchange(): return lax.all_to_all(array, 'tok', split_axis=0, concat_axis=0, tiled=True)  35.2 us
    ppermute x8, starting transfers between devices, send(): return lax.ppermute(value, 'seq', pairs)  20.7 us
    all_to_all x2, starting transfers between devices, exchange(): return lax.all_to_all(array, 'tok', split_axis=0, concat_axis=0, tiled=True)  14.4 us
    ppermute x8, waiting for transfers between devices, send(): return lax.ppermute(value, 'seq', pairs)  10.9 us
    pallas_call x2, Pallas kernels, attend(): pl.pallas_call(functools.partial(attend_kernel, min(256, total), head), g...  6.59 us
    pallas_call x2, Pallas kernels, pack(): pl.pallas_call(functools.partial(pack_kernel, count), out_shape=jax.Shape...  4.75 us
  transfers between devices with their start and end apart: 10, of which 6 were waited for; matrix products, arithmetic and copies ran while one was open for 2% of the time, Pallas kernels for 7%

profile of v2, /device:TPU:1, one launch (start us, length us, event | category | flops | bytes accessed | tf_op | source)
XLA Modules:
  0.0 147.1 jit_solution(10168151872652933414)
XLA Ops:
  0.6 2.4 %pack.3 = bf16[8,2,128,256]{3,2,1,0:T(8,128)(2,1)} custom-call(bf16[128,2048]{1,0:T(8,128)(2,1)} %refs_0_.3, bf16[128,2048]{1,0:T(8,128)(2,1)} %refs_1_.3), custom_call_target="tpu_custom_call" | custom-call | bytes 2097152 | tf_op jit(solution)/shard_map/pack/pallas_call | solution.py:83
  3.0 10.9 %all-to-all-start.1 = ((bf16[8,2,128,256]{3,2,1,0:T(8,128)(2,1)}), bf16[8,2,128,256]{3,2,1,0:T(8,128)(2,1)S(1)}, u32[]{:S(2)}, u32[]{:S(2)}) async-start(bf16[8,2,128,256]{3,2,1,0:T(8,128)(2,1)} %pack.3), calls=%async_computation.1 | async-start | bytes 2097152 | tf_op jit(solution)/shard_map/all_to_all | solution.py:313
  13.9 2.4 %pack.2 = bf16[8,2,128,256]{3,2,1,0:T(8,128)(2,1)} custom-call(bf16[128,2048]{1,0:T(8,128)(2,1)} %refs_0_.2, bf16[128,2048]{1,0:T(8,128)(2,1)} %refs_1_.2), custom_call_target="tpu_custom_call" | custom-call | bytes 2097152 | tf_op jit(solution)/shard_map/pack/pallas_call | solution.py:83
  16.3 0.0 copy-start.3
  16.3 0.0 copy-start
  16.3 0.0 copy-start.1
  16.3 26.8 %all-to-all-done.1.both_ref.qo_ref = bf16[8,2,128,256]{3,2,1,0:T(8,128)(2,1)S(1)} async-done(((bf16[8,2,128,256]{3,2,1,0:T(8,128)(2,1)}), bf16[8,2,128,256]{3,2,1,0:T(8,128)(2,1)S(1)}, u32[]{:S(2)}, u32[]{:S(2)}) %all-to-all-start.1) | async-done | bytes 1048608 | tf_op jit(solution)/shard_map/all_to_all | solution.py:313
  43.1 3.6 %all-to-all-start = ((bf16[8,2,128,256]{3,2,1,0:T(8,128)(2,1)}), bf16[8,2,128,256]{3,2,1,0:T(8,128)(2,1)S(1)}, u32[]{:S(2)}, u32[]{:S(2)}) async-start(bf16[8,2,128,256]{3,2,1,0:T(8,128)(2,1)} %pack.2), calls=%async_computation | async-start | bytes 2097152 | tf_op jit(solution)/shard_map/all_to_all | solution.py:313
  46.6 0.0 copy-done.3
  46.7 0.1 divide_bitcast_fusion.gates_ref
  46.7 0.0 copy-done
  46.7 0.0 copy-done.1
  46.7 2.0 %memory_read.1 = (f32[2,136,128]{2,1,0:T(8,128)S(1)}, f32[1024,256]{1,0:T(8,128)S(1)}) custom-call(f32[1,2]{1,0:T(1,128)S(1)} %divide_bitcast_fusion.gates_ref, bf16[8,2,128,256]{3,2,1,0:T(8,128)(2,1)S(1)} %all-to-all-done.1.both_ref.qo_ref, f32[2,128,128]{2,1,0:T(8,128)S(1)} %bitcast.12, f32[2,1,128]{2,1,0:T(1,128)S(1)} %bitcast.13), custom_call_target="tpu_custom_call" | custom-call | flops 1207959552 | bytes 4000000 | tf_op jit(solution)/shard_map/memory_read/pallas_call | solution.py:151
  48.7 2.4 %collective-permute-start = (f32[136,128]{1,0:T(8,128)S(1)}, f32[136,128]{1,0:T(8,128)S(1)}, u32[]{:S(2)}, u32[]{:S(2)}) collective-permute-start(f32[136,128]{1,0:T(8,128)S(1)} %select_bitcast_fusion), channel_id=1, source_target_pairs={{0,8},{8,0},{16,24},{24,16},{32,40},{40,32},{48,56},{56,48},{64,72... | collective-permute-start | bytes 208904 | tf_op jit(solution)/shard_map/ppermute | solution.py:279
  51.1 0.9 collective-permute-done
  52.0 1.3 collective-permute-start.1
  53.3 4.0 %collective-permute-done.1 = f32[136,128]{1,0:T(8,128)S(1)} collective-permute-done((f32[136,128]{1,0:T(8,128)S(1)}, f32[136,128]{1,0:T(8,128)S(1)}, u32[]{:S(2)}, u32[]{:S(2)}) %collective-permute-start.1) | collective-permute-done | bytes 69664 | tf_op jit(solution)/shard_map/ppermute | solution.py:279
  57.4 0.6 add.51
  58.0 1.3 collective-permute-start.2
  59.4 5.1 %collective-permute-done.2 = f32[136,128]{1,0:T(8,128)} collective-permute-done((f32[136,128]{1,0:T(8,128)}, f32[136,128]{1,0:T(8,128)}, u32[]{:S(2)}, u32[]{:S(2)}) %collective-permute-start.2) | collective-permute-done | bytes 69664 | tf_op jit(solution)/shard_map/ppermute | solution.py:279
  64.5 1.5 %fusion.1 = (f32[136,128]{1,0:T(8,128)}, f32[136,128]{1,0:T(8,128)}) fusion(f32[136,128]{1,0:T(8,128)S(1)} %bitcast_add_fusion, f32[136,128]{1,0:T(8,128)S(1)} %collective-permute-done.1, f32[136,128]{1,0:T(8,128)} %collective-permute-done.2), kind=kLoop, calls=%fused_computation.12 | loop fusion | flops 34816 | bytes 348160 | tf_op jit(solution)/shard_map/add | solution.py:291
  66.0 1.3 collective-permute-start.3
  67.3 8.5 %all-to-all-done.kv_ref = bf16[8,2,128,256]{3,2,1,0:T(8,128)(2,1)S(1)} async-done(((bf16[8,2,128,256]{3,2,1,0:T(8,128)(2,1)}), bf16[8,2,128,256]{3,2,1,0:T(8,128)(2,1)S(1)}, u32[]{:S(2)}, u32[]{:S(2)}) %all-to-all-start) | async-done | bytes 1048608 | tf_op jit(solution)/shard_map/all_to_all | solution.py:313
  75.8 0.0 copy-start.2
  75.8 3.3 %attend.2 = (bf16[1024,128]{1,0:T(8,128)(2,1)S(1)}, f32[1024,128]{1,0:T(8,128)S(1)}, f32[1024,128]{1,0:T(8,128)S(1)}) custom-call(f32[1,2]{1,0:T(1,128)S(1)} %divide_bitcast_fusion.gates_ref, bf16[8,2,128,256]{3,2,1,0:T(8,128)(2,1)S(1)} %all-to-all-done.1.both_ref.qo_ref, bf16[8,2,128,256]{3,2,1,0:T(8,128)(2,1)S(1)} %all-to-all-done.kv_ref, ...), custom_call_target="tpu_custom_call" | custom-call | flops 2147483648 | bytes 4000000 | tf_op jit(solution)/shard_map/attend/pallas_call | solution.py:219
  79.1 0.0 collective-permute-done.3
  79.1 0.0 copy-done.2
  79.2 4.7 %collective-permute-start.5 = (f32[136,128]{1,0:T(8,128)S(1)}, f32[136,128]{1,0:T(8,128)S(1)}, u32[]{:S(2)}, u32[]{:S(2)}) collective-permute-start(f32[136,128]{1,0:T(8,128)S(1)} %get-tuple-element.25), channel_id=1, source_target_pairs={{0,32},{8,40},{16,48},{24,56},{32,0},{40,8},{48,16},{56,24},{64,96... | collective-permute-start | bytes 208904 | tf_op jit(solution)/shard_map/ppermute | solution.py:279
  83.8 2.2 %collective-permute-start.6 = (f32[136,128]{1,0:T(8,128)S(1)}, f32[136,128]{1,0:T(8,128)S(1)}, u32[]{:S(2)}, u32[]{:S(2)}) collective-permute-start(f32[136,128]{1,0:T(8,128)S(1)} %get-tuple-element.26), channel_id=1, source_target_pairs={{0,16},{8,24},{16,32},{24,40},{32,48},{40,56},{48,0},{56,8},{64,80... | collective-permute-start | bytes 208904 | tf_op jit(solution)/shard_map/ppermute | solution.py:279
  86.0 4.3 %collective-permute-start.4 = (f32[136,128]{1,0:T(8,128)S(1)}, f32[136,128]{1,0:T(8,128)S(1)}, u32[]{:S(2)}, u32[]{:S(2)}) collective-permute-start(f32[136,128]{1,0:T(8,128)S(1)} %get-tuple-element.21), channel_id=1, source_target_pairs={{0,48},{8,56},{16,0},{24,8},{32,16},{40,24},{48,32},{56,40},{64,11... | collective-permute-start | bytes 208904 | tf_op jit(solution)/shard_map/ppermute | solution.py:279
  90.3 3.3 %attend.3 = (bf16[1024,128]{1,0:T(8,128)(2,1)S(1)}, f32[1024,128]{1,0:T(8,128)S(1)}, f32[1024,128]{1,0:T(8,128)S(1)}) custom-call(f32[1,2]{1,0:T(1,128)S(1)} %divide_bitcast_fusion.gates_ref, bf16[8,2,128,256]{3,2,1,0:T(8,128)(2,1)S(1)} %all-to-all-done.1.both_ref.qo_ref, bf16[8,2,128,256]{3,2,1,0:T(8,128)(2,1)S(1)} %all-to-all-done.kv_ref, ...), custom_call_target="tpu_custom_call" | custom-call | flops 2147483648 | bytes 4000000 | tf_op jit(solution)/shard_map/attend/pallas_call | solution.py:219
  93.6 0.0 collective-permute-done.5
  93.6 0.0 collective-permute-done.6
  93.6 0.0 collective-permute-done.4
  93.7 3.2 %collective-permute-start.7 = (f32[136,128]{1,0:T(8,128)S(1)}, f32[136,128]{1,0:T(8,128)S(1)}, u32[]{:S(2)}, u32[]{:S(2)}) collective-permute-start(f32[136,128]{1,0:T(8,128)S(1)} %get-tuple-element.19), channel_id=1, source_target_pairs={{0,8},{8,0},{16,24},{24,16},{32,40},{40,32},{48,56},{56,48},{64,72... | collective-permute-start | bytes 208904 | tf_op jit(solution)/shard_map/ppermute | solution.py:279
  97.0 0.9 collective-permute-done.7
  97.8 0.9 memory_write.1
  98.8 45.6 %all_to_all.15.source = bf16[8,3,128,256]{3,2,1,0:T(8,128)(2,1)} all-to-all(bf16[8,3,128,256]{3,2,1,0:T(8,128)(2,1)S(1)} %memory_write.1), channel_id=1, replica_groups=mesh['seq'=64,'tok'=8] {'tok'}, dimensions={0} | all-to-all | bytes 3145728 | tf_op jit(solution)/shard_map/all_to_all | solution.py:313
  144.4 2.7 %unpack.1 = (bf16[128,2048]{1,0:T(8,128)(2,1)}, bf16[128,2048]{1,0:T(8,128)(2,1)}, bf16[128,2048]{1,0:T(8,128)(2,1)}) custom-call(bf16[8,3,128,256]{3,2,1,0:T(8,128)(2,1)} %all_to_all.15.source), custom_call_target="tpu_custom_call" | custom-call | bytes 3145728 | tf_op jit(solution)/shard_map/unpack/pallas_call | solution.py:115
  (7 shorter events, 0.1 us)
Async XLA Ops:
  3.0 40.1 %all-to-all-start.1 = ((bf16[8,2,128,256]{3,2,1,0:T(8,128)(2,1)}), bf16[8,2,128,256]{3,2,1,0:T(8,128)(2,1)S(1)}, u32[]{:S(2)}, u32[]{:S(2)}) async-start(bf16[8,2,128,256]{3,2,1,0:T(8,128)(2,1)} %pack.3), calls=%async_computation.1 | async-start | bytes 2097152 | tf_op jit(solution)/shard_map/all_to_all | solution.py:313
  16.3 30.4 %copy-start.3 = (f32[16]{0:T(128)S(1)}, f32[16]{0:T(128)}, u32[]{:S(2)}) copy-start(f32[16]{0:T(128)} %param.13) | copy-start | bytes 196
  16.3 30.5 %copy-start = (f32[1,2,128,128]{3,2,1,0:T(8,128)S(1)}, f32[1,2,128,128]{3,2,1,0:T(8,128)}, u32[]{:S(2)}) copy-start(f32[1,2,128,128]{3,2,1,0:T(8,128)} %param.11) | copy-start | bytes 393220
  16.3 30.4 %copy-start.1 = (f32[1,2,128]{2,1,0:T(2,128)S(1)}, f32[1,2,128]{2,1,0:T(2,128)}, u32[]{:S(2)}) copy-start(f32[1,2,128]{2,1,0:T(2,128)} %param.12) | copy-start | bytes 3076
  43.1 32.7 %all-to-all-start = ((bf16[8,2,128,256]{3,2,1,0:T(8,128)(2,1)}), bf16[8,2,128,256]{3,2,1,0:T(8,128)(2,1)S(1)}, u32[]{:S(2)}, u32[]{:S(2)}) async-start(bf16[8,2,128,256]{3,2,1,0:T(8,128)(2,1)} %pack.2), calls=%async_computation | async-start | bytes 2097152 | tf_op jit(solution)/shard_map/all_to_all | solution.py:313
  48.7 3.3 %collective-permute-start = (f32[136,128]{1,0:T(8,128)S(1)}, f32[136,128]{1,0:T(8,128)S(1)}, u32[]{:S(2)}, u32[]{:S(2)}) collective-permute-start(f32[136,128]{1,0:T(8,128)S(1)} %select_bitcast_fusion), channel_id=1, source_target_pairs={{0,8},{8,0},{16,24},{24,16},{32,40},{40,32},{48,56},{56,48},{64,72... | collective-permute-start | bytes 208904 | tf_op jit(solution)/shard_map/ppermute | solution.py:279
  52.0 5.3 %collective-permute-start.1 = (f32[136,128]{1,0:T(8,128)S(1)}, f32[136,128]{1,0:T(8,128)S(1)}, u32[]{:S(2)}, u32[]{:S(2)}) collective-permute-start(f32[136,128]{1,0:T(8,128)S(1)} %bitcast_add_fusion), channel_id=1, source_target_pairs={{64,0},{72,8},{80,16},{88,24},{96,32},{104,40},{112,48},{120,56},{... | collective-permute-start | bytes 208904 | tf_op jit(solution)/shard_map/ppermute | solution.py:279
  58.0 6.4 %collective-permute-start.2 = (f32[136,128]{1,0:T(8,128)}, f32[136,128]{1,0:T(8,128)}, u32[]{:S(2)}, u32[]{:S(2)}) collective-permute-start(f32[136,128]{1,0:T(8,128)} %add.51), channel_id=1, source_target_pairs={{128,0},{136,8},{144,16},{152,24},{160,32},{168,40},{176,48},{184,... | collective-permute-start | bytes 208904 | tf_op jit(solution)/shard_map/ppermute | solution.py:279
  66.0 13.1 %collective-permute-start.3 = (f32[136,128]{1,0:T(8,128)}, f32[136,128]{1,0:T(8,128)S(1)}, u32[]{:S(2)}, u32[]{:S(2)}) collective-permute-start(f32[136,128]{1,0:T(8,128)} %get-tuple-element.23), channel_id=1, source_target_pairs={{256,0},{264,8},{272,16},{280,24},{288,32},{296,40},{304,48},{312,... | collective-permute-start | bytes 208904 | tf_op jit(solution)/shard_map/ppermute | solution.py:279
  75.8 3.3 %copy-start.2 = (f32[136,128]{1,0:T(8,128)S(1)}, f32[136,128]{1,0:T(8,128)}, u32[]{:S(2)}) copy-start(f32[136,128]{1,0:T(8,128)} %get-tuple-element.24) | copy-start | bytes 208900
  79.2 14.5 %collective-permute-start.5 = (f32[136,128]{1,0:T(8,128)S(1)}, f32[136,128]{1,0:T(8,128)S(1)}, u32[]{:S(2)}, u32[]{:S(2)}) collective-permute-start(f32[136,128]{1,0:T(8,128)S(1)} %get-tuple-element.25), channel_id=1, source_target_pairs={{0,32},{8,40},{16,48},{24,56},{32,0},{40,8},{48,16},{56,24},{64,96... | collective-permute-start | bytes 208904 | tf_op jit(solution)/shard_map/ppermute | solution.py:279
  83.8 9.8 %collective-permute-start.6 = (f32[136,128]{1,0:T(8,128)S(1)}, f32[136,128]{1,0:T(8,128)S(1)}, u32[]{:S(2)}, u32[]{:S(2)}) collective-permute-start(f32[136,128]{1,0:T(8,128)S(1)} %get-tuple-element.26), channel_id=1, source_target_pairs={{0,16},{8,24},{16,32},{24,40},{32,48},{40,56},{48,0},{56,8},{64,80... | collective-permute-start | bytes 208904 | tf_op jit(solution)/shard_map/ppermute | solution.py:279
  86.0 7.6 %collective-permute-start.4 = (f32[136,128]{1,0:T(8,128)S(1)}, f32[136,128]{1,0:T(8,128)S(1)}, u32[]{:S(2)}, u32[]{:S(2)}) collective-permute-start(f32[136,128]{1,0:T(8,128)S(1)} %get-tuple-element.21), channel_id=1, source_target_pairs={{0,48},{8,56},{16,0},{24,8},{32,16},{40,24},{48,32},{56,40},{64,11... | collective-permute-start | bytes 208904 | tf_op jit(solution)/shard_map/ppermute | solution.py:279
  93.7 4.1 %collective-permute-start.7 = (f32[136,128]{1,0:T(8,128)S(1)}, f32[136,128]{1,0:T(8,128)S(1)}, u32[]{:S(2)}, u32[]{:S(2)}) collective-permute-start(f32[136,128]{1,0:T(8,128)S(1)} %get-tuple-element.19), channel_id=1, source_target_pairs={{0,8},{8,0},{16,24},{24,16},{32,40},{40,32},{48,56},{56,48},{64,72... | collective-permute-start | bytes 208904 | tf_op jit(solution)/shard_map/ppermute | solution.py:279

commit v3 on v2

--- a/solution.py
+++ b/solution.py
@@ -295,7 +295,7 @@
     column = (me // 2) % columns
     whole = chip + below
     later = below
-    for shift in range(1, columns):
+    for shift in sorted(range(1, columns), key=lambda k: -min(k, columns - k)):
         value = jnp.where(column >= shift, whole, below)
         pairs = [
             ((r * columns + c) * 2 + k, (r * columns + (c - shift) % columns) * 2 + k)

time: 150 us -> 149 us (level)
  the two profiles are of different devices: /device:TPU:1 before, /device:TPU:30 now
where the time goes in v3:
time: 149 us; the launch traced here: 148 us
  waiting for transfers between devices  48.5 us (33%)
  blocking collectives  47.3 us (32%)
  starting transfers between devices  32.4 us (22%)
  Pallas kernels  17 us (11%)
  other arithmetic  2.38 us (2%)
    all_to_all x1, blocking collectives, exchange(): return lax.all_to_all(array, 'tok', split_axis=0, concat_axis=0, tiled=True)  47.3 us
    all_to_all x2, waiting for transfers between devices, exchange(): return lax.all_to_all(array, 'tok', split_axis=0, concat_axis=0, tiled=True)  30.6 us
    ppermute x8, starting transfers between devices, send(): return lax.ppermute(value, 'seq', pairs)  18.6 us
    ppermute x8, waiting for transfers between devices, send(): return lax.ppermute(value, 'seq', pairs)  17.8 us
    all_to_all x2, starting transfers between devices, exchange(): return lax.all_to_all(array, 'tok', split_axis=0, concat_axis=0, tiled=True)  13.9 us
    pallas_call x2, Pallas kernels, attend(): pl.pallas_call(functools.partial(attend_kernel, min(256, total), head), g...  6.59 us
    pallas_call x2, Pallas kernels, pack(): pl.pallas_call(functools.partial(pack_kernel, count), out_shape=jax.Shape...  4.75 us
  transfers between devices with their start and end apart: 10, of which 8 were waited for; matrix products, arithmetic and copies ran while one was open for 2% of the time, Pallas kernels for 7%

profile of v3, /device:TPU:30, one launch (start us, length us, event | category | flops | bytes accessed | tf_op | source)
XLA Modules:
  0.0 148.4 jit_solution(9645137902362097941)
XLA Ops:
  0.6 2.4 %pack.3 = bf16[8,2,128,256]{3,2,1,0:T(8,128)(2,1)} custom-call(bf16[128,2048]{1,0:T(8,128)(2,1)} %refs_0_.3, bf16[128,2048]{1,0:T(8,128)(2,1)} %refs_1_.3), custom_call_target="tpu_custom_call" | custom-call | bytes 2097152 | tf_op jit(solution)/shard_map/pack/pallas_call | solution.py:83
  3.0 10.3 %all-to-all-start.1 = ((bf16[8,2,128,256]{3,2,1,0:T(8,128)(2,1)}), bf16[8,2,128,256]{3,2,1,0:T(8,128)(2,1)S(1)}, u32[]{:S(2)}, u32[]{:S(2)}) async-start(bf16[8,2,128,256]{3,2,1,0:T(8,128)(2,1)} %pack.3), calls=%async_computation.1 | async-start | bytes 2097152 | tf_op jit(solution)/shard_map/all_to_all | solution.py:313
  13.3 2.4 %pack.2 = bf16[8,2,128,256]{3,2,1,0:T(8,128)(2,1)} custom-call(bf16[128,2048]{1,0:T(8,128)(2,1)} %refs_0_.2, bf16[128,2048]{1,0:T(8,128)(2,1)} %refs_1_.2), custom_call_target="tpu_custom_call" | custom-call | bytes 2097152 | tf_op jit(solution)/shard_map/pack/pallas_call | solution.py:83
  15.7 0.0 copy-start.3
  15.7 0.0 copy-start
  15.7 0.0 copy-start.1
  15.8 26.3 %all-to-all-done.1.both_ref.qo_ref = bf16[8,2,128,256]{3,2,1,0:T(8,128)(2,1)S(1)} async-done(((bf16[8,2,128,256]{3,2,1,0:T(8,128)(2,1)}), bf16[8,2,128,256]{3,2,1,0:T(8,128)(2,1)S(1)}, u32[]{:S(2)}, u32[]{:S(2)}) %all-to-all-start.1) | async-done | bytes 1048608 | tf_op jit(solution)/shard_map/all_to_all | solution.py:313
  42.1 3.6 %all-to-all-start = ((bf16[8,2,128,256]{3,2,1,0:T(8,128)(2,1)}), bf16[8,2,128,256]{3,2,1,0:T(8,128)(2,1)S(1)}, u32[]{:S(2)}, u32[]{:S(2)}) async-start(bf16[8,2,128,256]{3,2,1,0:T(8,128)(2,1)} %pack.2), calls=%async_computation | async-start | bytes 2097152 | tf_op jit(solution)/shard_map/all_to_all | solution.py:313
  45.6 0.0 copy-done.3
  45.6 0.1 divide_bitcast_fusion.gates_ref
  45.7 0.0 copy-done
  45.7 0.0 copy-done.1
  45.7 2.0 %memory_read.1 = (f32[2,136,128]{2,1,0:T(8,128)S(1)}, f32[1024,256]{1,0:T(8,128)S(1)}) custom-call(f32[1,2]{1,0:T(1,128)S(1)} %divide_bitcast_fusion.gates_ref, bf16[8,2,128,256]{3,2,1,0:T(8,128)(2,1)S(1)} %all-to-all-done.1.both_ref.qo_ref, f32[2,128,128]{2,1,0:T(8,128)S(1)} %bitcast.12, f32[2,1,128]{2,1,0:T(1,128)S(1)} %bitcast.13), custom_call_target="tpu_custom_call" | custom-call | flops 1207959552 | bytes 4000000 | tf_op jit(solution)/shard_map/memory_read/pallas_call | solution.py:151
  47.7 1.9 %collective-permute-start = (f32[136,128]{1,0:T(8,128)S(1)}, f32[136,128]{1,0:T(8,128)S(1)}, u32[]{:S(2)}, u32[]{:S(2)}) collective-permute-start(f32[136,128]{1,0:T(8,128)S(1)} %select_bitcast_fusion), channel_id=1, source_target_pairs={{0,8},{8,0},{16,24},{24,16},{32,40},{40,32},{48,56},{56,48},{64,72... | collective-permute-start | bytes 208904 | tf_op jit(solution)/shard_map/ppermute | solution.py:279
  49.6 1.2 collective-permute-done
  50.9 2.4 %collective-permute-start.1 = (f32[136,128]{1,0:T(8,128)S(1)}, f32[136,128]{1,0:T(8,128)S(1)}, u32[]{:S(2)}, u32[]{:S(2)}) collective-permute-start(f32[136,128]{1,0:T(8,128)S(1)} %bitcast_add_fusion), channel_id=1, source_target_pairs={{64,0},{72,8},{80,16},{88,24},{96,32},{104,40},{112,48},{120,56},{... | collective-permute-start | bytes 208904 | tf_op jit(solution)/shard_map/ppermute | solution.py:279
  53.3 5.0 %collective-permute-done.1 = f32[136,128]{1,0:T(8,128)S(1)} collective-permute-done((f32[136,128]{1,0:T(8,128)S(1)}, f32[136,128]{1,0:T(8,128)S(1)}, u32[]{:S(2)}, u32[]{:S(2)}) %collective-permute-start.1) | collective-permute-done | bytes 69664 | tf_op jit(solution)/shard_map/ppermute | solution.py:279
  58.3 0.6 add.51
  58.9 1.9 %collective-permute-start.2 = (f32[136,128]{1,0:T(8,128)}, f32[136,128]{1,0:T(8,128)}, u32[]{:S(2)}, u32[]{:S(2)}) collective-permute-start(f32[136,128]{1,0:T(8,128)} %add.51), channel_id=1, source_target_pairs={{128,0},{136,8},{144,16},{152,24},{160,32},{168,40},{176,48},{184,... | collective-permute-start | bytes 208904 | tf_op jit(solution)/shard_map/ppermute | solution.py:279
  60.9 6.7 %collective-permute-done.2 = f32[136,128]{1,0:T(8,128)} collective-permute-done((f32[136,128]{1,0:T(8,128)}, f32[136,128]{1,0:T(8,128)}, u32[]{:S(2)}, u32[]{:S(2)}) %collective-permute-start.2) | collective-permute-done | bytes 69664 | tf_op jit(solution)/shard_map/ppermute | solution.py:279
  67.6 1.5 %fusion.1 = (f32[136,128]{1,0:T(8,128)}, f32[136,128]{1,0:T(8,128)}) fusion(f32[136,128]{1,0:T(8,128)S(1)} %bitcast_add_fusion, f32[136,128]{1,0:T(8,128)S(1)} %collective-permute-done.1, f32[136,128]{1,0:T(8,128)} %collective-permute-done.2), kind=kLoop, calls=%fused_computation.12 | loop fusion | flops 34816 | bytes 348160 | tf_op jit(solution)/shard_map/add | solution.py:291
  69.1 1.3 collective-permute-start.3
  70.4 4.3 %all-to-all-done.kv_ref = bf16[8,2,128,256]{3,2,1,0:T(8,128)(2,1)S(1)} async-done(((bf16[8,2,128,256]{3,2,1,0:T(8,128)(2,1)}), bf16[8,2,128,256]{3,2,1,0:T(8,128)(2,1)S(1)}, u32[]{:S(2)}, u32[]{:S(2)}) %all-to-all-start) | async-done | bytes 1048608 | tf_op jit(solution)/shard_map/all_to_all | solution.py:313
  74.8 0.0 copy-start.2
  74.8 3.3 %attend.2 = (bf16[1024,128]{1,0:T(8,128)(2,1)S(1)}, f32[1024,128]{1,0:T(8,128)S(1)}, f32[1024,128]{1,0:T(8,128)S(1)}) custom-call(f32[1,2]{1,0:T(1,128)S(1)} %divide_bitcast_fusion.gates_ref, bf16[8,2,128,256]{3,2,1,0:T(8,128)(2,1)S(1)} %all-to-all-done.1.both_ref.qo_ref, bf16[8,2,128,256]{3,2,1,0:T(8,128)(2,1)S(1)} %all-to-all-done.kv_ref, ...), custom_call_target="tpu_custom_call" | custom-call | flops 2147483648 | bytes 4000000 | tf_op jit(solution)/shard_map/attend/pallas_call | solution.py:219
  78.1 1.4 collective-permute-done.3
  79.5 0.0 copy-done.2
  79.5 2.7 %collective-permute-start.5 = (f32[136,128]{1,0:T(8,128)S(1)}, f32[136,128]{1,0:T(8,128)S(1)}, u32[]{:S(2)}, u32[]{:S(2)}) collective-permute-start(f32[136,128]{1,0:T(8,128)S(1)} %get-tuple-element.25), channel_id=1, source_target_pairs={{0,48},{8,56},{16,0},{24,8},{32,16},{40,24},{48,32},{56,40},{64,11... | collective-permute-start | bytes 208904 | tf_op jit(solution)/shard_map/ppermute | solution.py:279
  82.2 4.3 %collective-permute-start.6 = (f32[136,128]{1,0:T(8,128)S(1)}, f32[136,128]{1,0:T(8,128)S(1)}, u32[]{:S(2)}, u32[]{:S(2)}) collective-permute-start(f32[136,128]{1,0:T(8,128)S(1)} %get-tuple-element.26), channel_id=1, source_target_pairs={{0,16},{8,24},{16,32},{24,40},{32,48},{40,56},{48,0},{56,8},{64,80... | collective-permute-start | bytes 208904 | tf_op jit(solution)/shard_map/ppermute | solution.py:279
  86.6 2.1 %collective-permute-start.4 = (f32[136,128]{1,0:T(8,128)S(1)}, f32[136,128]{1,0:T(8,128)S(1)}, u32[]{:S(2)}, u32[]{:S(2)}) collective-permute-start(f32[136,128]{1,0:T(8,128)S(1)} %get-tuple-element.21), channel_id=1, source_target_pairs={{0,32},{8,40},{16,48},{24,56},{32,0},{40,8},{48,16},{56,24},{64,96... | collective-permute-start | bytes 208904 | tf_op jit(solution)/shard_map/ppermute | solution.py:279
  88.7 3.3 %attend.3 = (bf16[1024,128]{1,0:T(8,128)(2,1)S(1)}, f32[1024,128]{1,0:T(8,128)S(1)}, f32[1024,128]{1,0:T(8,128)S(1)}) custom-call(f32[1,2]{1,0:T(1,128)S(1)} %divide_bitcast_fusion.gates_ref, bf16[8,2,128,256]{3,2,1,0:T(8,128)(2,1)S(1)} %all-to-all-done.1.both_ref.qo_ref, bf16[8,2,128,256]{3,2,1,0:T(8,128)(2,1)S(1)} %all-to-all-done.kv_ref, ...), custom_call_target="tpu_custom_call" | custom-call | flops 2147483648 | bytes 4000000 | tf_op jit(solution)/shard_map/attend/pallas_call | solution.py:219
  92.0 0.0 collective-permute-done.5
  92.0 0.0 collective-permute-done.6
  92.0 2.3 %collective-permute-done.4 = f32[136,128]{1,0:T(8,128)S(1)} collective-permute-done((f32[136,128]{1,0:T(8,128)S(1)}, f32[136,128]{1,0:T(8,128)S(1)}, u32[]{:S(2)}, u32[]{:S(2)}) %collective-permute-start.4) | collective-permute-done | bytes 69664 | tf_op jit(solution)/shard_map/ppermute | solution.py:279
  94.3 1.9 %collective-permute-start.7 = (f32[136,128]{1,0:T(8,128)S(1)}, f32[136,128]{1,0:T(8,128)S(1)}, u32[]{:S(2)}, u32[]{:S(2)}) collective-permute-start(f32[136,128]{1,0:T(8,128)S(1)} %get-tuple-element.19), channel_id=1, source_target_pairs={{0,8},{8,0},{16,24},{24,16},{32,40},{40,32},{48,56},{56,48},{64,72... | collective-permute-start | bytes 208904 | tf_op jit(solution)/shard_map/ppermute | solution.py:279
  96.3 1.2 collective-permute-done.7
  97.5 0.9 memory_write.1
  98.4 47.3 %all_to_all.15.source = bf16[8,3,128,256]{3,2,1,0:T(8,128)(2,1)} all-to-all(bf16[8,3,128,256]{3,2,1,0:T(8,128)(2,1)S(1)} %memory_write.1), channel_id=1, replica_groups=mesh['seq'=64,'tok'=8] {'tok'}, dimensions={0} | all-to-all | bytes 3145728 | tf_op jit(solution)/shard_map/all_to_all | solution.py:313
  145.7 2.7 %unpack.1 = (bf16[128,2048]{1,0:T(8,128)(2,1)}, bf16[128,2048]{1,0:T(8,128)(2,1)}, bf16[128,2048]{1,0:T(8,128)(2,1)}) custom-call(bf16[8,3,128,256]{3,2,1,0:T(8,128)(2,1)} %all_to_all.15.source), custom_call_target="tpu_custom_call" | custom-call | bytes 3145728 | tf_op jit(solution)/shard_map/unpack/pallas_call | solution.py:115
  (7 shorter events, 0.1 us)
Async XLA Ops:
  3.0 39.1 %all-to-all-start.1 = ((bf16[8,2,128,256]{3,2,1,0:T(8,128)(2,1)}), bf16[8,2,128,256]{3,2,1,0:T(8,128)(2,1)S(1)}, u32[]{:S(2)}, u32[]{:S(2)}) async-start(bf16[8,2,128,256]{3,2,1,0:T(8,128)(2,1)} %pack.3), calls=%async_computation.1 | async-start | bytes 2097152 | tf_op jit(solution)/shard_map/all_to_all | solution.py:313
  15.7 29.9 %copy-start.3 = (f32[16]{0:T(128)S(1)}, f32[16]{0:T(128)}, u32[]{:S(2)}) copy-start(f32[16]{0:T(128)} %param.13) | copy-start | bytes 196
  15.7 30.0 %copy-start = (f32[1,2,128,128]{3,2,1,0:T(8,128)S(1)}, f32[1,2,128,128]{3,2,1,0:T(8,128)}, u32[]{:S(2)}) copy-start(f32[1,2,128,128]{3,2,1,0:T(8,128)} %param.11) | copy-start | bytes 393220
  15.7 30.0 %copy-start.1 = (f32[1,2,128]{2,1,0:T(2,128)S(1)}, f32[1,2,128]{2,1,0:T(2,128)}, u32[]{:S(2)}) copy-start(f32[1,2,128]{2,1,0:T(2,128)} %param.12) | copy-start | bytes 3076
  42.1 32.7 %all-to-all-start = ((bf16[8,2,128,256]{3,2,1,0:T(8,128)(2,1)}), bf16[8,2,128,256]{3,2,1,0:T(8,128)(2,1)S(1)}, u32[]{:S(2)}, u32[]{:S(2)}) async-start(bf16[8,2,128,256]{3,2,1,0:T(8,128)(2,1)} %pack.2), calls=%async_computation | async-start | bytes 2097152 | tf_op jit(solution)/shard_map/all_to_all | solution.py:313
  47.7 3.2 %collective-permute-start = (f32[136,128]{1,0:T(8,128)S(1)}, f32[136,128]{1,0:T(8,128)S(1)}, u32[]{:S(2)}, u32[]{:S(2)}) collective-permute-start(f32[136,128]{1,0:T(8,128)S(1)} %select_bitcast_fusion), channel_id=1, source_target_pairs={{0,8},{8,0},{16,24},{24,16},{32,40},{40,32},{48,56},{56,48},{64,72... | collective-permute-start | bytes 208904 | tf_op jit(solution)/shard_map/ppermute | solution.py:279
  50.9 7.4 %collective-permute-start.1 = (f32[136,128]{1,0:T(8,128)S(1)}, f32[136,128]{1,0:T(8,128)S(1)}, u32[]{:S(2)}, u32[]{:S(2)}) collective-permute-start(f32[136,128]{1,0:T(8,128)S(1)} %bitcast_add_fusion), channel_id=1, source_target_pairs={{64,0},{72,8},{80,16},{88,24},{96,32},{104,40},{112,48},{120,56},{... | collective-permute-start | bytes 208904 | tf_op jit(solution)/shard_map/ppermute | solution.py:279
  58.9 8.7 %collective-permute-start.2 = (f32[136,128]{1,0:T(8,128)}, f32[136,128]{1,0:T(8,128)}, u32[]{:S(2)}, u32[]{:S(2)}) collective-permute-start(f32[136,128]{1,0:T(8,128)} %add.51), channel_id=1, source_target_pairs={{128,0},{136,8},{144,16},{152,24},{160,32},{168,40},{176,48},{184,... | collective-permute-start | bytes 208904 | tf_op jit(solution)/shard_map/ppermute | solution.py:279
  69.1 10.3 %collective-permute-start.3 = (f32[136,128]{1,0:T(8,128)}, f32[136,128]{1,0:T(8,128)S(1)}, u32[]{:S(2)}, u32[]{:S(2)}) collective-permute-start(f32[136,128]{1,0:T(8,128)} %get-tuple-element.23), channel_id=1, source_target_pairs={{256,0},{264,8},{272,16},{280,24},{288,32},{296,40},{304,48},{312,... | collective-permute-start | bytes 208904 | tf_op jit(solution)/shard_map/ppermute | solution.py:279
  74.8 4.7 %copy-start.2 = (f32[136,128]{1,0:T(8,128)S(1)}, f32[136,128]{1,0:T(8,128)}, u32[]{:S(2)}) copy-start(f32[136,128]{1,0:T(8,128)} %get-tuple-element.24) | copy-start | bytes 208900
  79.5 12.5 %collective-permute-start.5 = (f32[136,128]{1,0:T(8,128)S(1)}, f32[136,128]{1,0:T(8,128)S(1)}, u32[]{:S(2)}, u32[]{:S(2)}) collective-permute-start(f32[136,128]{1,0:T(8,128)S(1)} %get-tuple-element.25), channel_id=1, source_target_pairs={{0,48},{8,56},{16,0},{24,8},{32,16},{40,24},{48,32},{56,40},{64,11... | collective-permute-start | bytes 208904 | tf_op jit(solution)/shard_map/ppermute | solution.py:279
  82.2 9.7 %collective-permute-start.6 = (f32[136,128]{1,0:T(8,128)S(1)}, f32[136,128]{1,0:T(8,128)S(1)}, u32[]{:S(2)}, u32[]{:S(2)}) collective-permute-start(f32[136,128]{1,0:T(8,128)S(1)} %get-tuple-element.26), channel_id=1, source_target_pairs={{0,16},{8,24},{16,32},{24,40},{32,48},{40,56},{48,0},{56,8},{64,80... | collective-permute-start | bytes 208904 | tf_op jit(solution)/shard_map/ppermute | solution.py:279
  86.6 7.7 %collective-permute-start.4 = (f32[136,128]{1,0:T(8,128)S(1)}, f32[136,128]{1,0:T(8,128)S(1)}, u32[]{:S(2)}, u32[]{:S(2)}) collective-permute-start(f32[136,128]{1,0:T(8,128)S(1)} %get-tuple-element.21), channel_id=1, source_target_pairs={{0,32},{8,40},{16,48},{24,56},{32,0},{40,8},{48,16},{56,24},{64,96... | collective-permute-start | bytes 208904 | tf_op jit(solution)/shard_map/ppermute | solution.py:279
  94.3 3.2 %collective-permute-start.7 = (f32[136,128]{1,0:T(8,128)S(1)}, f32[136,128]{1,0:T(8,128)S(1)}, u32[]{:S(2)}, u32[]{:S(2)}) collective-permute-start(f32[136,128]{1,0:T(8,128)S(1)} %get-tuple-element.19), channel_id=1, source_target_pairs={{0,8},{8,0},{16,24},{24,16},{32,40},{40,32},{48,56},{56,48},{64,72... | collective-permute-start | bytes 208904 | tf_op jit(solution)/shard_map/ppermute | solution.py:279
